TPU v7x, 32 devices: a whole 2x2x4 slice. The times are simulated.
32 devices in a mesh: seq: 16 (over z, x, core), batch: 2 (over y).
Axes of the slice: x: 2, y: 2, z: 4, core: 2. Of those that a mesh axis runs over, the one named last changes fastest.
Arguments:
- tokens: bfloat16 [4, 2048, 768], P('batch', 'seq'), may hold values from -6 to 6
- cotangent: bfloat16 [4, 2048, 768], P('batch', 'seq'), may hold values from -6 to 6
- gains: float32 [2, 768], replicated, may hold values from 0.5 to 1.5
- mixing: bfloat16 [3, 768, 192], P(None, ('seq', 'batch')), may hold values from -0.4375 to 0.4375
- twiddle: bfloat16 [3, 192, 4, 4], replicated, may hold values from -3 to 3
- expand: bfloat16 [2, 768, 768], P(None, ('seq', 'batch')), may hold values from -0.4375 to 0.4375
- spread: bfloat16 [2, 768, 4, 4], replicated, may hold values from -3 to 3
- shrink: bfloat16 [3072, 192], P(('seq', 'batch')), may hold values from -0.21875 to 0.21875
- squeeze: bfloat16 [192, 4, 4], replicated, may hold values from -3 to 3
- kernel: float32 [3, 1536], replicated, may hold values from -3 to 3
- lifting: float32 [5, 128], replicated, may hold values from -16 to 16
- phases: float32 [128], replicated, may hold values from -3.140625 to 3.140625
- mapping: float32 [128, 128], replicated, may hold values from -1 to 1
- readout: float32 [128, 768], replicated, may hold values from -0.09375 to 0.09375
- damping: float32 [768], replicated, may hold values from 0.00048828125 to 0.03
Outputs:
- layer_output: bfloat16 [4, 2048, 768], P('batch', 'seq')
- tokens_grad: float32 [4, 2048, 768], P('batch', 'seq')
- gains_grad: float32 [2, 768], replicated
- mixing_grad: float32 [3, 768, 192], P(None, ('seq', 'batch'))
- twiddle_grad: float32 [3, 192, 4, 4], replicated
- expand_grad: float32 [2, 768, 768], P(None, ('seq', 'batch'))
- spread_grad: float32 [2, 768, 4, 4], replicated
- shrink_grad: float32 [3072, 192], P(('seq', 'batch'))
- squeeze_grad: float32 [192, 4, 4], replicated
- kernel_grad: float32 [3, 1536], replicated
- lifting_grad: float32 [5, 128], replicated
- phases_grad: float32 [128], replicated
- mapping_grad: float32 [128, 128], replicated
- readout_grad: float32 [128, 768], replicated
All inputs are finite; a program needn't handle non-finite values.
Results may differ from a plain program's by a relative error of at most 0.012.
Values may be sent and summed in bfloat16 or wider, within the bound.
No kernel may reach another device: no remote copies, remote signals or barrier semaphores. Data moves between devices by JAX's collectives and lax.ppermute only.
A program may use at most 448 MiB of HBM per device.

v0:
```python
import math

import jax
import jax.numpy as jnp
from jax import lax
from jax.sharding import PartitionSpec as P

BLOCKS = 4


HIGHEST = lax.Precision.HIGHEST


def shifted(value, axis, steps):
    count = lax.axis_size(axis)
    first, last = (max(0, -steps), min(count, count - steps))
    return lax.ppermute(value, axis, [(source, source + steps) for source in range(first, last)])


def features(length):
    positions = jnp.arange(length, dtype=jnp.int32)
    columns = [positions.astype(jnp.float32) / length]
    for harmonic in (1, 2):
        phase_now = 2.0 * math.pi / length * (harmonic * positions % length).astype(jnp.float32)
        columns.append(jnp.cos(phase_now))
        columns.append(jnp.sin(phase_now))
    return jnp.stack(columns, 1)


def make_filter(lifting, phases, mapping, readout, damping, length):
    positions = jnp.arange(length, dtype=jnp.int32).astype(jnp.float32)
    layer_one = jnp.sin(jnp.dot(features(length), lifting, precision=HIGHEST) + phases)
    layer_two = jnp.sin(jnp.dot(layer_one, mapping, precision=HIGHEST))
    return jnp.dot(layer_two, readout, precision=HIGHEST) * jnp.exp(
        -positions[:, None] * damping[None, :]
    )


def dft_tables(modulus, columns):
    bins = jnp.arange(modulus, dtype=jnp.int32)[:, None]
    places = jnp.arange(columns, dtype=jnp.int32)[None, :]
    phase_now = 2.0 * math.pi / modulus * (bins * places % modulus).astype(jnp.float32)
    return (jnp.cos(phase_now), jnp.sin(phase_now))


def normalize(values):
    average = jnp.mean(values, -1, keepdims=True)
    centred = values - average
    variance = jnp.mean(centred * centred, -1, keepdims=True)
    factor = lax.rsqrt(variance + 1e-05)
    return (centred * factor, factor)


def norm_back(upstream, normed, factor):
    mean_plain = jnp.mean(upstream, -1, keepdims=True)
    mean_joint = jnp.mean(upstream * normed, -1, keepdims=True)
    return factor * (upstream - mean_plain - normed * mean_joint)


def first_factor(rounded, inner):
    row_count = rounded.shape[0]
    width_in = inner.shape[0] // BLOCKS
    return jnp.einsum(
        "rai,aij->raj",
        rounded.reshape(row_count, BLOCKS, width_in),
        inner.reshape(BLOCKS, width_in, inner.shape[1]),
        preferred_element_type=jnp.float32,
    )


def second_factor(sectioned, outer):
    mixed = jnp.einsum("raj,jab->rbj", sectioned, outer, precision=HIGHEST)
    return mixed.reshape(sectioned.shape[0], -1)


def monarch_back(upstream, rounded, sectioned, inner, outer):
    row_count = upstream.shape[0]
    width_out = outer.shape[0]
    width_in = inner.shape[0] // BLOCKS
    shaped = upstream.reshape(row_count, BLOCKS, width_out)
    sectioned_grad = jnp.einsum("rbj,jab->raj", shaped, outer, precision=HIGHEST).astype(
        jnp.bfloat16
    )
    outer_grad = jnp.einsum("raj,rbj->jab", sectioned, shaped, precision=HIGHEST)
    blocks = inner.reshape(BLOCKS, width_in, width_out)
    input_grad = jnp.einsum(
        "raj,aij->rai", sectioned_grad, blocks, preferred_element_type=jnp.float32
    )
    inner_grad = jnp.einsum(
        "rai,raj->aij",
        rounded.reshape(row_count, BLOCKS, width_in),
        sectioned_grad,
        preferred_element_type=jnp.float32,
    )
    return (
        input_grad.reshape(row_count, -1),
        inner_grad.reshape(BLOCKS * width_in, width_out),
        outer_grad,
    )


def short_conv(extended, taps):
    return taps[0] * extended[:, 2:] + taps[1] * extended[:, 1:-1] + taps[2] * extended[:, :-2]


def conv_back(later, taps):
    return taps[0] * later[:, :-2] + taps[1] * later[:, 1:-1] + taps[2] * later[:, 2:]


def taps_grad(extended, grad_rows):
    return jnp.stack(
        [
            jnp.sum(extended[:, 2:] * grad_rows, (0, 1)),
            jnp.sum(extended[:, 1:-1] * grad_rows, (0, 1)),
            jnp.sum(extended[:, :-2] * grad_rows, (0, 1)),
        ]
    )


def per_device(
    tokens,
    cotangent,
    gains,
    mixing,
    twiddle,
    expand,
    spread,
    shrink,
    squeeze,
    kernel,
    lifting,
    phases,
    mapping,
    readout,
    damping,
):
    seq_count, share_len, width = tokens.shape
    row_count = seq_count * share_len
    pieces_all = lax.axis_size("seq")
    place = lax.axis_index("seq")
    length = pieces_all * share_len
    doubled = 2 * share_len
    mixing_full, expand_full, shrink_full = (
        lax.all_gather(mixing, ("seq", "batch"), axis=1, tiled=True),
        lax.all_gather(expand, ("seq", "batch"), axis=1, tiled=True),
        lax.all_gather(shrink, ("seq", "batch"), axis=0, tiled=True),
    )
    twiddle_wide = twiddle.astype(jnp.float32)
    spread_wide = spread.astype(jnp.float32)
    squeeze_wide = squeeze.astype(jnp.float32)
    cos_half, sin_half = dft_tables(doubled, share_len)
    cos_full, sin_full = dft_tables(doubled, doubled)

    def spectra_of(lifting_now, phases_now, mapping_now, readout_now, damping_now):
        response = make_filter(
            lifting_now, phases_now, mapping_now, readout_now, damping_now, length
        )
        segments = response.reshape(pieces_all, share_len, readout_now.shape[1])
        earlier = jnp.concatenate(
            [jnp.zeros((1, share_len, readout_now.shape[1]), jnp.float32), segments[:-1]], 0
        )
        circular = jnp.concatenate(
            [
                segments,
                jnp.zeros((pieces_all, 1, readout_now.shape[1]), jnp.float32),
                earlier[:, 1:],
            ],
            1,
        )
        real_part = jnp.einsum("fm,kmd->kfd", cos_full, circular, precision=HIGHEST)
        imaginary = -jnp.einsum("fm,kmd->kfd", sin_full, circular, precision=HIGHEST)
        return (real_part, imaginary)

    def full_spectra(lifting_now, phases_now, mapping_now, readout_now):
        return spectra_of(lifting_now, phases_now, mapping_now, readout_now, damping)

    def transform(signal_now):
        grouped = signal_now.astype(jnp.float32).reshape(
            signal_now.shape[0], -1, share_len, signal_now.shape[2]
        )
        real_part = jnp.einsum("fn,smnd->smfd", cos_half, grouped, precision=HIGHEST)
        imaginary = -jnp.einsum("fn,smnd->smfd", sin_half, grouped, precision=HIGHEST)
        return (real_part, imaginary)

    def inverse(real_part, imaginary):
        return jnp.einsum("fn,sfd->snd", cos_half, real_part, precision=HIGHEST) - jnp.einsum(
            "fn,sfd->snd", sin_half, imaginary, precision=HIGHEST
        )

    def select_filter(lags):
        live_mask = (lags >= 0).astype(jnp.float32)[:, None, None]
        lag_index = jnp.clip(lags, 0, pieces_all - 1)
        return (
            jnp.take(filt_real, lag_index, axis=0) * live_mask,
            jnp.take(filt_imag, lag_index, axis=0) * live_mask,
            live_mask,
            lag_index,
        )

    inputs = tokens.astype(jnp.float32).reshape(row_count, width)
    normed_one, factor_one = normalize(inputs)
    rounded_one = (normed_one * gains[0]).astype(jnp.bfloat16)
    sectioned_signal = first_factor(rounded_one, mixing_full[0])
    signal = (
        second_factor(sectioned_signal, twiddle_wide[0])
        .astype(jnp.bfloat16)
        .reshape(seq_count, share_len, width)
    )
    sectioned_switch = first_factor(rounded_one, mixing_full[1])
    switch = (
        second_factor(sectioned_switch, twiddle_wide[1])
        .astype(jnp.bfloat16)
        .reshape(seq_count, share_len, width)
    )
    prior_signal, prior_switch = shifted(
        (signal[:, share_len - 2 :], switch[:, share_len - 2 :]), "seq", 1
    )
    signal_ext = jnp.concatenate([prior_signal, signal], 1).astype(jnp.float32)
    switch_ext = jnp.concatenate([prior_switch, switch], 1).astype(jnp.float32)
    conv_in = short_conv(signal_ext, kernel[:, :width]).astype(jnp.bfloat16)
    gate_seq = short_conv(switch_ext, kernel[:, width:])
    empty = jnp.zeros((seq_count, doubled, width), jnp.float32)
    (filt_real, filt_imag), filter_pull = jax.vjp(full_spectra, lifting, phases, mapping, readout)
    own_real, own_imag = transform(conv_in)
    real_part, imaginary = transform(lax.all_gather(conv_in, "seq", axis=1, tiled=True))
    totals = (empty, empty)
    lags = place - jnp.arange(real_part.shape[1], dtype=jnp.int32)
    kern_real, kern_imag, live_mask, lag_index = select_filter(lags)
    new_real = totals[0] + jnp.sum(kern_real[None] * real_part - kern_imag[None] * imaginary, 1)
    new_imag = totals[1] + jnp.sum(kern_real[None] * imaginary + kern_imag[None] * real_part, 1)
    sum_real = new_real
    sum_imag = new_imag
    long_out = inverse(sum_real, sum_imag) / doubled
    gated = (gate_seq * long_out).astype(jnp.bfloat16).reshape(row_count, width)
    sectioned_merge = first_factor(gated, mixing_full[2])
    residual = inputs + second_factor(sectioned_merge, twiddle_wide[2])
    normed_two, factor_two = normalize(residual)
    rounded_two = (normed_two * gains[1]).astype(jnp.bfloat16)
    sectioned_gate = first_factor(rounded_two, expand_full[0])
    gate_pre = second_factor(sectioned_gate, spread_wide[0])
    sectioned_up = first_factor(rounded_two, expand_full[1])
    up_pre = second_factor(sectioned_up, spread_wide[1])
    activated, gelu_pull = jax.vjp(jax.nn.gelu, gate_pre)
    hidden = (activated * up_pre).astype(jnp.bfloat16)
    sectioned_down = first_factor(hidden, shrink_full)
    layer = residual + second_factor(sectioned_down, squeeze_wide)
    layer_output = layer.astype(jnp.bfloat16).reshape(seq_count, share_len, width)
    upstream = cotangent.astype(jnp.float32).reshape(row_count, width)
    hidden_grad, shrink_grad, squeeze_grad = monarch_back(
        upstream, hidden, sectioned_down, shrink_full, squeeze_wide
    )
    gate_grad = gelu_pull(hidden_grad * up_pre)[0]
    up_grad = hidden_grad * activated
    from_gate, expand_gate, spread_gate = monarch_back(
        gate_grad, rounded_two, sectioned_gate, expand_full[0], spread_wide[0]
    )
    from_up, expand_up, spread_up = monarch_back(
        up_grad, rounded_two, sectioned_up, expand_full[1], spread_wide[1]
    )
    rounded_two_grad = from_gate + from_up
    gain_two_grad = jnp.sum(rounded_two_grad * normed_two, 0)
    residual_grad = upstream + norm_back(rounded_two_grad * gains[1], normed_two, factor_two)
    gated_grad, mixing_merge, twiddle_merge = monarch_back(
        residual_grad, gated, sectioned_merge, mixing_full[2], twiddle_wide[2]
    )
    gated_grad = gated_grad.reshape(seq_count, share_len, width)
    long_grad = (gated_grad * gate_seq).astype(jnp.bfloat16)
    switch_grad = (gated_grad * long_out).astype(jnp.bfloat16)
    zero_filter = jnp.zeros((pieces_all, doubled, width), jnp.float32)
    real_part, imaginary = transform(lax.all_gather(long_grad, "seq", axis=1, tiled=True))
    totals = (empty, empty, zero_filter, zero_filter)
    collect_real_part = real_part / doubled
    collect_imaginary = imaginary / doubled
    lags = jnp.arange(collect_real_part.shape[1], dtype=jnp.int32) - place
    kern_real, kern_imag, live_mask, lag_index = select_filter(lags)
    new_real = totals[0] + jnp.sum(
        kern_real[None] * collect_real_part + kern_imag[None] * collect_imaginary, 1
    )
    new_imag = totals[1] + jnp.sum(
        kern_real[None] * collect_imaginary - kern_imag[None] * collect_real_part, 1
    )
    prod_real = jnp.sum(own_real * collect_real_part + own_imag * collect_imaginary, 0) * live_mask
    prod_imag = jnp.sum(own_real * collect_imaginary - own_imag * collect_real_part, 0) * live_mask
    resp_real = totals[2].at[lag_index].add(prod_real)
    resp_imag = totals[3].at[lag_index].add(prod_imag)
    conv_grad = inverse(new_real, new_imag).astype(jnp.bfloat16)
    lifting_grad, phases_grad, mapping_grad, readout_grad = filter_pull((resp_real, resp_imag))
    next_signal, next_switch = shifted((conv_grad[:, :2], switch_grad[:, :2]), "seq", -1)
    signal_later = jnp.concatenate([conv_grad, next_signal], 1).astype(jnp.float32)
    switch_later = jnp.concatenate([switch_grad, next_switch], 1).astype(jnp.float32)
    signal_grad = conv_back(signal_later, kernel[:, :width]).reshape(row_count, width)
    switch_back = conv_back(switch_later, kernel[:, width:]).reshape(row_count, width)
    kernel_grad = jnp.concatenate(
        [
            taps_grad(signal_ext, conv_grad.astype(jnp.float32)),
            taps_grad(switch_ext, switch_grad.astype(jnp.float32)),
        ],
        1,
    )
    from_signal, mixing_signal, twiddle_signal = monarch_back(
        signal_grad, rounded_one, sectioned_signal, mixing_full[0], twiddle_wide[0]
    )
    from_switch, mixing_switch, twiddle_switch = monarch_back(
        switch_back, rounded_one, sectioned_switch, mixing_full[1], twiddle_wide[1]
    )
    rounded_one_grad = from_signal + from_switch
    gain_one_grad = jnp.sum(rounded_one_grad * normed_one, 0)
    tokens_grad = residual_grad + norm_back(rounded_one_grad * gains[0], normed_one, factor_one)
    mixing_grad = jnp.stack([mixing_signal, mixing_switch, mixing_merge])
    expand_grad = jnp.stack([expand_gate, expand_up])
    mixing_owned, expand_owned, shrink_owned = (
        lax.psum_scatter(mixing_grad, ("seq", "batch"), scatter_dimension=1, tiled=True),
        lax.psum_scatter(expand_grad, ("seq", "batch"), scatter_dimension=1, tiled=True),
        lax.psum_scatter(shrink_grad, ("seq", "batch"), scatter_dimension=0, tiled=True),
    )
    summed = lax.psum(
        (
            jnp.stack([gain_one_grad, gain_two_grad]),
            jnp.stack([twiddle_signal, twiddle_switch, twiddle_merge]),
            jnp.stack([spread_gate, spread_up]),
            squeeze_grad,
            kernel_grad,
            lifting_grad,
            phases_grad,
            mapping_grad,
            readout_grad,
        ),
        ("seq", "batch"),
    )
    return (
        layer_output,
        tokens_grad.reshape(seq_count, share_len, width),
        summed[0],
        mixing_owned,
        summed[1],
        expand_owned,
        summed[2],
        shrink_owned,
        summed[3],
        summed[4],
        summed[5],
        summed[6],
        summed[7],
        summed[8],
    )


def solution(mesh):
    return jax.shard_map(
        per_device,
        mesh=mesh,
        in_specs=(
            P("batch", "seq", None),
            P("batch", "seq", None),
            P(),
            P(None, ("seq", "batch"), None),
            P(),
            P(None, ("seq", "batch"), None),
            P(),
            P(("seq", "batch"), None),
            P(),
            P(),
            P(),
            P(),
            P(),
            P(),
            P(),
        ),
        out_specs=(
            P("batch", "seq", None),
            P("batch", "seq", None),
            P(),
            P(None, ("seq", "batch"), None),
            P(),
            P(None, ("seq", "batch"), None),
            P(),
            P(("seq", "batch"), None),
            P(),
            P(),
            P(),
            P(),
            P(),
            P(),
        ),
        check_vma=False,
    )
```

profile of v0, /device:TPU:1, one launch (start us, length us, event | category | flops | bytes accessed | tf_op | source)
XLA Modules:
  0.0 1313.8 jit_solution(2780601016876033855)
XLA Ops:
  14.5 74.1 %all_gather.15 = bf16[3,768,192]{2,1,0:T(8,128)(2,1)S(1)} all-gather(bf16[3,24,192]{2,1,0:T(8,128)(2,1)S(1)} %copy-done.100), channel_id=1, replica_groups=mesh['seq'=16,'batch'=2] {'seq','batch'}, dimensions={1}, use_global_device_ids=true | all-gather | bytes 912384 | tf_op jit(solution)/shard_map/all_gather | solution.py:144
  137.1 6.7 copy.457
  151.0 15.7 %fusion.24 = f32[16,256,768]{1,2,0:T(8,128)} fusion(f32[16,127,768]{1,2,0:T(8,128)S(1)} %pad_slice_fusion.1, f32[16,128,768]{1,2,0:T(8,128)S(1)} %bitcast.362, f32[256]{0:T(256)S(1)} %pad.34.clone), kind=kOutput, calls=%fused_computation.59 | convolution fusion | flops 9670885376 | bytes 25117696 | tf_op jit(solution)/shard_map/jvp(fm,kmd->kfd)/dot_general | solution.py:170
  166.6 10.6 gather_fusion
  177.2 17.7 %negate_bitcast_fusion = f32[16,256,768]{1,2,0:T(8,128)} fusion(f32[16,127,768]{1,2,0:T(8,128)} %copy-done.3, f32[16,128,768]{1,2,0:T(8,128)} %copy.457, f32[256]{0:T(256)S(1)} %pad.34.clone), kind=kOutput, calls=%fused_computation.43 | convolution fusion | flops 9674031104 | bytes 25117696 | tf_op jit(solution)/shard_map/jvp(fm,kmd->kfd)/dot_general | solution.py:171
  194.9 10.6 gather_fusion.1
  207.4 19.0 %select_multiply_fusion.3 = (f32[16,256,768]{1,2,0:T(8,128)}, f32[16,256,768]{1,2,0:T(8,128)}) fusion(f32[16,256,768]{1,2,0:T(8,128)} %gather_fusion, f32[16]{0:T(128)S(1)} %compare_convert_fusion.1, pred[16]{0:T(512)(128)(4,1)S(1)} %compare_and_fusion.1, f32[16,256,768]{1,2,0:T(8,128)} %gather_fusion.1), kind=kLoop, calls=%fused_computation.40 | loop fusion | flops 12582912 | bytes 50331728 | tf_op jit(solution)/shard_map/mul | solution.py:194
  243.6 17.7 %fusion.114 = f32[2,16,768,256]{3,2,1,0:T(8,128)} fusion(bf16[2,16,128,768]{3,2,1,0:T(8,128)(2,1)} %bitcast.363), kind=kOutput, calls=%fused_computation.222 | convolution fusion | flops 9664135168 | bytes 31457280 | tf_op jit(solution)/shard_map/fn,smnd->smfd/dot_general | solution.py:182
  261.4 24.9 %fusion.11 = (f32[2,256,768]{1,2,0:T(8,128)}, f32[2,256,768]{1,2,0:T(8,128)}) fusion(f32[2,16,768,256]{3,2,1,0:T(8,128)} %fusion.114, f32[16,256,768]{1,2,0:T(8,128)} %get-tuple-element.155, f32[16,256,768]{1,2,0:T(8,128)} %get-tuple-element.154, bf16[2,16,128,768]{3,2,1,0:T(8,128)(2,1)S(1)} %bitcast.366), kind=kOutput, calls=%fused_computation.27 | convolution fusion | flops 9719971840 | bytes 59768832 | tf_op jit(solution)/shard_map/fn,smnd->smfd/dot_general | solution.py:181
  326.0 10.1 fusion.32
  337.9 7.0 fusion.37
  370.0 10.7 gather_fusion.2
  380.7 10.6 gather_fusion.3
  391.8 19.5 %fusion.17 = (f32[16,256,768]{1,2,0:T(8,128)}, f32[16,256,768]{1,2,0:T(8,128)}) fusion(f32[16,256,768]{1,2,0:T(8,128)} %gather_fusion.2, f32[16]{0:T(128)S(1)} %compare_convert_fusion, pred[16]{0:T(512)(128)(4,1)S(1)} %compare_and_fusion, f32[16,256,768]{1,2,0:T(8,128)} %gather_fusion.3), kind=kLoop, calls=%fused_computation.38 | loop fusion | flops 18874368 | bytes 50331728 | tf_op jit(solution)/shard_map/mul | solution.py:277
  434.9 18.1 %fusion.112 = f32[2,16,768,256]{3,2,1,0:T(8,128)} fusion(bf16[2,16,128,768]{3,2,1,0:T(8,128)(2,1)} %bitcast.359), kind=kOutput, calls=%fused_computation.220 | convolution fusion | flops 9664135168 | bytes 31457280 | tf_op jit(solution)/shard_map/fn,smnd->smfd/dot_general | solution.py:182
  453.0 41.5 %fusion.5 = (f32[16,256,768]{1,2,0:T(8,128)}, f32[16,256,768]{1,2,0:T(8,128)}, f32[2,256,768]{1,2,0:T(8,128)}, f32[2,256,768]{1,2,0:T(8,128)}) fusion(f32[2,16,768,256]{3,2,1,0:T(8,128)} %fusion.112, f32[2,256,768]{1,2,0:T(8,128)S(1)} %multiply_bitcast_fusion, f32[2,256,768]{1,2,0:T(8,128)S(1)} %copy-done.47, f32[16,256,768]{1,2,0:T(8,128)} %get-tuple-element.151, ...), kind=kOutput, calls=%fused_computation.15 | convolution fusion | flops 9764012032 | bytes 88080384 | tf_op jit(solution)/shard_map/fn,smnd->smfd/dot_general | solution.py:181
  494.5 18.6 %broadcast_multiply_fusion.1 = (f32[16,256,768]{1,2,0:T(8,128)}, f32[16,256,768]{1,2,0:T(8,128)}) fusion(f32[16,256,768]{1,2,0:T(8,128)} %get-tuple-element.89, f32[16]{0:T(128)S(1)} %copy-done.120, f32[16,256,768]{1,2,0:T(8,128)} %get-tuple-element.90), kind=kLoop, calls=%fused_computation.52 | loop fusion | flops 6291456 | bytes 50331712 | tf_op jit(solution)/shard_map/mul | solution.py:283
  513.1 12.7 copy.549
  525.8 12.6 copy.551
  544.3 28.6 %scatter_fusion.1 = f32[16,256,768]{2,1,0:T(8,128)} fusion(f32[16,256,768]{2,1,0:T(8,128)} %broadcast_in_dim.11.clone, s32[16]{0:T(128)S(1)} %copy-done.118, f32[16,256,768]{2,1,0:T(8,128)} %copy.551), kind=kCustom, calls=%fused_computation.5 | custom fusion | flops 3145728 | bytes 37748800 | tf_op jit(solution)/shard_map/scatter-add | solution.py:284
  572.9 19.6 %fusion.12 = f32[16,768,256]{1,2,0:T(8,128)} fusion(f32[16,256,768]{2,1,0:T(8,128)} %scatter_fusion.1), kind=kOutput, calls=%fused_computation.31 | convolution fusion | flops 9664593920 | bytes 25165824 | tf_op jit(solution)/shard_map/transpose(jvp(fm,kmd->kfd))/dot_general | solution.py:170
  598.4 28.5 %scatter_fusion = f32[16,256,768]{2,1,0:T(8,128)} fusion(f32[16,256,768]{2,1,0:T(8,128)} %broadcast_in_dim.11.clone.1, s32[16]{0:T(128)S(1)} %copy-done.118, f32[16,256,768]{2,1,0:T(8,128)} %copy.549), kind=kCustom, calls=%fused_computation.4 | custom fusion | flops 3145728 | bytes 37748800 | tf_op jit(solution)/shard_map/scatter-add | solution.py:285
  626.9 21.5 %add_bitcast_fusion = f32[16,256,768]{2,1,0:T(8,128)} fusion(f32[16,768,256]{1,2,0:T(8,128)} %fusion.12, f32[16,256,768]{2,1,0:T(8,128)} %scatter_fusion), kind=kOutput, calls=%fused_computation.41 | convolution fusion | flops 9670885376 | bytes 37748736 | tf_op jit(solution)/shard_map/transpose(jvp(fm,kmd->kfd))/dot_general | solution.py:171
  669.7 8.2 convolution_multiply_fusion
  719.0 10.6 convolution_bitcast_fusion
  731.9 10.2 convolution_bitcast_fusion.1
  751.1 7.3 fusion.239
  780.8 54.7 %all-reduce.8.cloned.1.call-done = (f32[2,768]{1,0:T(2,128)}, f32[3,192,4,4]{1,3,2,0:T(4,128)}, f32[192,4,4]{2,1,0:T(4,128)}, f32[3,1536]{1,0:T(4,128)}, f32[5,128]{1,0:T(8,128)}, /*index=5*/f32[128]{0:T(128)}) async-done(((f32[2,768]{1,0:T(2,128)}, f32[3,192,4,4]{1,3,2,0:T(4,128)}, f32[192,4,4]{2,1,0:T(4,128)}, f32[3,1536]{1,0:T(4,128)}, f32[5,128]{1,0:T(8,128)}, /*index=5*/f32[128]{0:T(128)}), ...) | async-done | bytes 76816 | tf_op jit(solution)/shard_map/psum | solution.py:316
  837.3 104.7 %reduce-scatter.10.cloned.1.call-done = f32[96,192]{1,0:T(8,128)} async-done(((f32[3072,192]{1,0:T(8,128)}), f32[96,192]{1,0:T(8,128)}) %reduce-scatter.10.cloned.1.call-update) | async-done | bytes 73744
  942.0 113.1 %reduce-scatter.8.cloned.1.call-done = f32[2,24,768]{2,1,0:T(8,128)} async-done(((f32[2,768,768]{2,1,0:T(8,128)}), f32[2,24,768]{2,1,0:T(8,128)}) %reduce-scatter.8.cloned.1.call-update) | async-done | bytes 147472 | tf_op jit(solution)/shard_map/reduce_scatter | solution.py:313
  1055.1 136.3 %all-reduce.10.cloned.1.call-done = (f32[2,768,4,4]{1,3,2,0:T(4,128)}, f32[128,128]{1,0:T(8,128)}, f32[128,768]{1,0:T(8,128)}) async-done(((f32[2,768,4,4]{1,3,2,0:T(4,128)}, f32[128,128]{1,0:T(8,128)}, f32[128,768]{1,0:T(8,128)}), (f32[2,768,4,4]{1,3,2,0:T(4,128)}, f32[128,128]{1,0:T(8,128)}, f32[128,768]{1,0:T(8,128)})) %all-reduce.10.cloned.1.call-update) | async-done | bytes 557072 | tf_op jit(solution)/shard_map/psum | solution.py:316
  1191.4 104.2 %reduce-scatter.6.cloned.1.call-done = f32[3,24,192]{2,1,0:T(8,128)} async-done(((f32[3,768,192]{2,1,0:T(8,128)}), f32[3,24,192]{2,1,0:T(8,128)}) %reduce-scatter.6.cloned.1.call-update) | async-done | bytes 55312 | tf_op jit(solution)/shard_map/reduce_scatter | solution.py:312
  (463 shorter events, 291.8 us)
Async XLA Ops:
  7.2 113.0 %copy-start = (f32[128,768]{1,0:T(8,128)S(1)}, f32[128,768]{1,0:T(8,128)}, u32[]{:S(2)}) copy-start(f32[128,768]{1,0:T(8,128)} %param.30) | copy-start | bytes 1179652
  7.2 224.7 %all-gather.9.cloned.1.call-start = ((), (), s32[]{:S(2)}) async-start(), calls=%async_computation.5 | async-start | bytes 1622016 | tf_op jit(solution)/shard_map/all_gather | solution.py:146
  7.9 232.5 %all-gather.7.cloned.1.call-start = ((), (), s32[]{:S(2)}) async-start(), calls=%async_computation.4 | async-start | bytes 2433024 | tf_op jit(solution)/shard_map/all_gather | solution.py:145
  8.7 234.9 %all-gather.5.cloned.1.call-start = ((), (), s32[]{:S(2)}) async-start(), calls=%async_computation.3 | async-start | bytes 6684672 | tf_op jit(solution)/shard_map/all_gather | solution.py:225
  10.0 290.7 %copy-start.4 = (bf16[2,128,768]{1,0,2:T(2,128)(2,1)}, bf16[2,128,768]{1,0,2:T(2,128)(2,1)S(1)}, u32[]{:S(2)}) copy-start(bf16[2,128,768]{1,0,2:T(2,128)(2,1)S(1)} %copy.448) | copy-start | bytes 1179652
  10.3 79.6 %copy-start.20 = (f32[256,4,192]{0,2,1:T(8,128)}, f32[256,4,192]{0,2,1:T(8,128)S(1)}, u32[]{:S(2)}) copy-start(f32[256,4,192]{0,2,1:T(8,128)S(1)} %reshape.554) | copy-start | bytes 2359300
  11.1 78.8 %copy-start.98 = (f32[768]{0:T(1024)}, f32[768]{0:T(1024)S(1)}, u32[]{:S(2)}) copy-start(f32[768]{0:T(1024)S(1)} %get-tuple-element.112) | copy-start | bytes 9220
  11.1 217.3 %copy-start.96 = (f32[768]{0:T(1024)}, f32[768]{0:T(1024)S(1)}, u32[]{:S(2)}) copy-start(f32[768]{0:T(1024)S(1)} %get-tuple-element.111) | copy-start | bytes 9220
  11.2 78.7 %copy-start.88 = (f32[4,192]{1,0:T(4,128)}, f32[4,192]{1,0:T(4,128)S(1)}, u32[]{:S(2)}) copy-start(f32[4,192]{1,0:T(4,128)S(1)} %mul.712) | copy-start | bytes 9220
  12.1 77.7 %copy-start.69 = (bf16[1,192,4,4]{2,3,1,0:T(4,128)(2,1)}, bf16[1,192,4,4]{2,3,1,0:T(4,128)(2,1)S(1)}, u32[]{:S(2)}) copy-start(bf16[1,192,4,4]{2,3,1,0:T(4,128)(2,1)S(1)} %copy.611) | copy-start | bytes 18436
  13.0 76.9 %copy-start.108 = (f32[2,128]{1,0:T(2,128)}, f32[2,128]{1,0:T(2,128)S(1)}, u32[]{:S(2)}) copy-start(f32[2,128]{1,0:T(2,128)S(1)} %get-tuple-element.157) | copy-start | bytes 3076
  13.0 76.9 %copy-start.110 = (f32[256]{0:T(256)}, f32[256]{0:T(256)S(1)}, u32[]{:S(2)}) copy-start(f32[256]{0:T(256)S(1)} %get-tuple-element.156) | copy-start | bytes 3076
  14.3 75.6 %copy-start.112 = (f32[256]{0:T(256)}, f32[256]{0:T(256)S(1)}, u32[]{:S(2)}) copy-start(f32[256]{0:T(256)S(1)} %get-tuple-element.149) | copy-start | bytes 3076
  14.5 86.2 %copy-start.27 = (bf16[256,4,192]{0,2,1:T(8,128)(2,1)}, bf16[256,4,192]{0,2,1:T(8,128)(2,1)S(1)}, u32[]{:S(2)}) copy-start(bf16[256,4,192]{0,2,1:T(8,128)(2,1)S(1)} %multiply_convert_fusion.4) | copy-start | bytes 1179652
  93.2 5.2 collective-permute-start.1
  95.8 194.3 %copy-start.101 = (f32[768]{0:T(1024)}, f32[768]{0:T(1024)S(1)}, u32[]{:S(2)}) copy-start(f32[768]{0:T(1024)S(1)} %get-tuple-element.106) | copy-start | bytes 9220
  100.4 334.5 %all-gather.11.cloned.1.call-start = ((), (), s32[]{:S(2)}) async-start(), calls=%async_computation.6 | async-start | bytes 6684672 | tf_op jit(solution)/shard_map/all_gather | solution.py:270
  104.4 126.6 %collective-permute-start = (bf16[2,2,768]{2,1,0:T(2,128)(2,1)S(1)}, bf16[2,2,768]{2,1,0:T(2,128)(2,1)}, u32[]{:S(2)}, u32[]{:S(2)}) collective-permute-start(bf16[2,2,768]{2,1,0:T(2,128)(2,1)S(1)} %slice.192), channel_id=1, source_target_pairs={{0,2},{2,4},{4,6},{6,8},{8,10},{10,12},{12,14},{14,16},{16,18},{18... | collective-permute-start | bytes 18440 | tf_op jit(solution)/shard_map/ppermute | solution.py:17
  206.4 20.1 %copy-start.48 = (bf16[2,128,768]{1,0,2:T(2,128)(2,1)}, bf16[2,128,768]{1,0,2:T(2,128)(2,1)S(1)}, u32[]{:S(2)}) copy-start(bf16[2,128,768]{1,0,2:T(2,128)(2,1)S(1)} %copy.489) | copy-start | bytes 1179652
  206.6 19.7 %copy-start.78 = (bf16[256,4,192]{0,2,1:T(8,128)(2,1)}, bf16[256,4,192]{0,2,1:T(8,128)(2,1)S(1)}, u32[]{:S(2)}) copy-start(bf16[256,4,192]{0,2,1:T(8,128)(2,1)S(1)} %reshape_reshape.17) | copy-start | bytes 1179652
  207.3 24.5 %copy-start.73 = (bf16[192,4,256]{2,1,0:T(4,128)(2,1)}, bf16[192,4,256]{2,1,0:T(4,128)(2,1)S(1)}, u32[]{:S(2)}) copy-start(bf16[192,4,256]{2,1,0:T(4,128)(2,1)S(1)} %convolution_convert_fusion.5) | copy-start | bytes 1179652
  369.9 45.2 %copy-start.72 = (bf16[2,128,768]{2,1,0:T(8,128)(2,1)}, bf16[2,128,768]{2,1,0:T(8,128)(2,1)S(1)}, u32[]{:S(2)}) copy-start(bf16[2,128,768]{2,1,0:T(8,128)(2,1)S(1)} %get-tuple-element.122) | copy-start | bytes 1179652
  369.9 465.7 %all-reduce.8.cloned.1.call-start = ((), (), s32[]{:S(2)}) async-start(), calls=%async_computation.10 | async-start | bytes 955392 | tf_op jit(solution)/shard_map/psum | solution.py:316
  391.3 20.1 %copy-start.119 = (f32[16]{0:T(128)}, f32[16]{0:T(128)S(1)}, u32[]{:S(2)}) copy-start(f32[16]{0:T(128)S(1)} %compare_convert_fusion) | copy-start | bytes 196
  391.8 19.5 %copy-start.50 = (bf16[2,128,768]{2,1,0:T(8,128)(2,1)S(1)}, bf16[2,128,768]{2,1,0:T(8,128)(2,1)}, u32[]{:S(2)}) copy-start(bf16[2,128,768]{2,1,0:T(8,128)(2,1)} %add_convert_fusion.1) | copy-start | bytes 1179652
  415.7 17.2 %collective-permute-start.3 = (bf16[2,2,768]{2,1,0:T(2,128)(2,1)}, bf16[2,2,768]{2,1,0:T(2,128)(2,1)}, u32[]{:S(2)}, u32[]{:S(2)}) collective-permute-start(bf16[2,2,768]{2,1,0:T(2,128)(2,1)} %slice.208), channel_id=1, source_target_pairs={{2,0},{4,2},{6,4},{8,6},{10,8},{12,10},{14,12},{16,14},{18,16},{20... | collective-permute-start | bytes 18440 | tf_op jit(solution)/shard_map/ppermute | solution.py:17
  453.0 41.5 %copy-start.120 = (f32[16]{0:T(128)S(1)}, f32[16]{0:T(128)}, u32[]{:S(2)}) copy-start(f32[16]{0:T(128)} %copy-done.119) | copy-start | bytes 196
  667.2 17.8 %collective-permute-start.2 = (bf16[2,2,768]{2,1,0:T(2,128)(2,1)S(1)}, bf16[2,2,768]{2,1,0:T(2,128)(2,1)S(1)}, u32[]{:S(2)}, u32[]{:S(2)}) collective-permute-start(bf16[2,2,768]{2,1,0:T(2,128)(2,1)S(1)} %slice.204), channel_id=1, source_target_pairs={{2,0},{4,2},{6,4},{8,6},{10,8},{12,10},{14,12},{16,14},{18,16},{20... | collective-permute-start | bytes 18440 | tf_op jit(solution)/shard_map/ppermute | solution.py:17
  708.7 233.4 %reduce-scatter.10.cloned.1.call-start = ((), (), s32[]{:S(2)}) async-start(), calls=%async_computation.9 | async-start | bytes 3244032
  712.5 342.6 %reduce-scatter.8.cloned.1.call-start = ((), (), s32[]{:S(2)}) async-start(), calls=%async_computation.8 | async-start | bytes 4866048 | tf_op jit(solution)/shard_map/reduce_scatter | solution.py:313
  717.2 474.2 %all-reduce.10.cloned.1.call-start = ((), (), s32[]{:S(2)}) async-start(), calls=%async_computation.11 | async-start | bytes 1114112 | tf_op jit(solution)/shard_map/psum | solution.py:316
  758.4 537.2 %reduce-scatter.6.cloned.1.call-start = ((), (), s32[]{:S(2)}) async-start(), calls=%async_computation.7 | async-start | bytes 2433024 | tf_op jit(solution)/shard_map/reduce_scatter | solution.py:312
  (111 other events, 736.9 us)
Sparse Core Ops, SparseCore 0:
  10.9 58.7 all-gather.8
  72.7 56.4 all-gather.6
  132.1 60.8 all-gather.4
  370.0 58.7 all-gather.10
  708.8 126.7 all-reduce.7
  842.3 99.6 reduce-scatter.9
  949.0 106.0 reduce-scatter.7
  1061.9 129.4 all-reduce.9
  1198.1 97.4 reduce-scatter.5
where the time goes:
time: 1320 us; the launch traced here: 1310 us
  waiting for transfers between devices  517 us (39%)
  matrix products  338 us (26%)
  local copies, waits for them, and re-layouts  207 us (16%)
  other arithmetic  151 us (11%)
  blocking collectives  74.1 us (6%)
  between operations  16.1 us (1%)
    psum x2, waiting for transfers between devices, per_device(): lax.psum((jnp.stack([gain_one_grad, gain_two_grad]), jnp.stack([twiddle_s...  191 us
    reduce_scatter x1, waiting for transfers between devices, per_device(): lax.psum_scatter(expand_grad, ('seq', 'batch'), scatter_dimension=1, tile...  113 us
    unnamed x10, waiting for transfers between devices  106 us
    reduce_scatter x1, waiting for transfers between devices, per_device(): lax.psum_scatter(mixing_grad, ('seq', 'batch'), scatter_dimension=1, tile...  104 us
    all_gather x1, blocking collectives, per_device(): lax.all_gather(mixing, ('seq', 'batch'), axis=1, tiled=True)  74.1 us
    dot_general x3, matrix products, transform(): jnp.einsum('fn,smnd->smfd', cos_half, grouped, precision=HIGHEST)  68.9 us
    unnamed x279, local copies, waits for them, and re-layouts  41 us
    dot_general x2, matrix products, spectra_of(): jnp.einsum('fm,kmd->kfd', sin_full, circular, precision=HIGHEST)  39.2 us
  transfers between devices with their start and end apart: 13, of which 6 were waited for; matrix products, arithmetic and copies ran while one was open for 22% of the time, Pallas kernels for 0%

commit v1 on v0

v1 whole, which is shorter than its diff:
```python
import functools
import math

import jax
import jax.numpy as jnp
import numpy as np
from jax import lax
from jax.experimental import pallas as pl
from jax.experimental.pallas import tpu as pltpu
from jax.sharding import PartitionSpec as P

BLOCKS = 4
BOTH = ("seq", "batch")
F32 = jnp.float32
BF16 = jnp.bfloat16
HIGHEST = lax.Precision.HIGHEST
NN = ((1,), (0,))
NT = ((1,), (1,))
TN = ((0,), (0,))
ROUND_Z = (0, 4, 8, 12)
ROUND_XC = (0, 2, 1, 3)


def mm(left, right, dims=NN, precision=None):
    return lax.dot_general(
        left, right, (dims, ((), ())), preferred_element_type=F32, precision=precision
    )


def call(body, outs, operands, scratch=(), scalars=0, limit=48, flops=0):
    specs = [
        pl.BlockSpec(memory_space=pltpu.SMEM if k < scalars else pltpu.VMEM)
        for k in range(len(operands))
    ]
    return pl.pallas_call(
        body,
        out_shape=[jax.ShapeDtypeStruct(shape, kind) for shape, kind in outs],
        in_specs=specs,
        out_specs=[pl.BlockSpec(memory_space=pltpu.VMEM) for _ in outs],
        scratch_shapes=list(scratch),
        compiler_params=pltpu.CompilerParams(vmem_limit_bytes=limit << 20),
        cost_estimate=pl.CostEstimate(flops=int(flops), bytes_accessed=1 << 20, transcendentals=0),
    )(*operands)


def packed_tables(points):
    size = 2 * points
    place = np.arange(size)[:, None].astype(np.int64)
    bins = np.arange(points)[None, :]
    angle = 2.0 * np.pi / size * ((place * bins) % size)
    forward = np.concatenate([np.cos(angle), -np.sin(angle)], 1)
    forward[:, points] = np.where(np.arange(size) % 2 == 0, 1.0, -1.0)
    weight = np.where(np.arange(size) % points == 0, 1.0, 2.0) / size
    backward = (forward * weight[None, :]).T
    return forward.astype(np.float32), np.ascontiguousarray(backward).astype(np.float32)


def split_table(table):
    high = table.astype(jnp.bfloat16)
    low = (table - high.astype(np.float32)).astype(jnp.bfloat16)
    return high, low


def feature_rows(length):
    place = np.arange(length)
    rows = [place / length]
    for harmonic in (1, 2):
        angle = 2.0 * np.pi / length * ((harmonic * place) % length)
        rows += [np.cos(angle), np.sin(angle)]
    rows += [np.ones(length), np.zeros(length), np.zeros(length)]
    return np.stack(rows).astype(np.float32)


def spread_matrix(pieces, span):
    width = pieces * span
    out = np.zeros((BLOCKS, pieces, BLOCKS, span, width), np.float32)
    for b in range(BLOCKS):
        for piece in range(pieces):
            for k in range(span):
                out[b, piece, b, k, piece * span + k] = 1.0
    return out.reshape(BLOCKS, pieces * BLOCKS * span, width).astype(jnp.bfloat16)


def normalize_rows(values):
    centred = values - jnp.mean(values, -1, keepdims=True)
    factor = lax.rsqrt(jnp.mean(centred * centred, -1, keepdims=True) + 1e-05)
    return centred * factor, factor


def sincos(angle):
    turns = jnp.floor(angle * (2.0 / math.pi) + 0.5)
    rest = angle - turns * 1.5703125
    rest = rest - turns * 4.837512969970703125e-4
    rest = rest - turns * 7.54978995489188216e-8
    square = rest * rest
    sine = rest + rest * square * (
        -1.6666654611e-1 + square * (8.3321608736e-3 + square * -1.9515295891e-4)
    )
    cosine = (
        1.0
        - 0.5 * square
        + square
        * square
        * (4.166664568298827e-2 + square * (-1.388731625493765e-3 + square * 2.443315711809948e-5))
    )
    quarter = turns - 4.0 * jnp.floor(turns * 0.25)
    odd = (quarter == 1.0) | (quarter == 3.0)
    sine_sign = jnp.where(quarter >= 2.0, -1.0, 1.0)
    cosine_sign = jnp.where((quarter == 1.0) | (quarter == 2.0), -1.0, 1.0)
    return (
        jnp.where(odd, cosine, sine) * sine_sign,
        jnp.where(odd, sine, cosine) * cosine_sign,
    )


def parts_of(values):
    width = values.shape[1] // BLOCKS
    return [values[:, k * width : (k + 1) * width] for k in range(BLOCKS)]


def mix(sectioned, rows):
    return [
        sum(sectioned[a] * rows[4 * a + b : 4 * a + b + 1, :] for a in range(BLOCKS))
        for b in range(BLOCKS)
    ]


def unmix(upstream, rows):
    return [
        sum(upstream[b] * rows[4 * a + b : 4 * a + b + 1, :] for b in range(BLOCKS))
        for a in range(BLOCKS)
    ]


def mix_grad(sectioned, upstream):
    return jnp.concatenate(
        [
            jnp.sum(sectioned[a] * upstream[b], 0, keepdims=True)
            for a in range(BLOCKS)
            for b in range(BLOCKS)
        ],
        0,
    )


def lane_of(shape):
    return lax.broadcasted_iota(jnp.int32, shape, len(shape) - 1)


def row_of(shape):
    return lax.broadcasted_iota(jnp.int32, shape, 0)


def time_rows(block_ref, span):
    pieces, rows, _ = block_ref.shape
    return jnp.concatenate(
        [
            block_ref[n].astype(F32)[s * span : (s + 1) * span]
            for s in range(rows // span)
            for n in range(pieces)
        ],
        1,
    )


def later_lanes(values, steps, length):
    total = values.shape[1]
    moved = pltpu.roll(values, total - steps, 1)
    return jnp.where(lane_of(values.shape) % length < length - steps, moved, 0.0)


def earlier_lanes(values, steps, length):
    moved = pltpu.roll(values, steps, 1)
    return jnp.where(lane_of(values.shape) % length >= steps, moved, 0.0)


def to_blocks(lanes_now, out_ref, length):
    pieces, _, width = out_ref.shape
    seqs = lanes_now.shape[1] // length
    for n in range(pieces):
        out_ref[n] = jnp.concatenate(
            [
                lanes_now[:, s * length + n * width : s * length + (n + 1) * width]
                for s in range(seqs)
            ],
            0,
        ).astype(BF16)


def spectrum(block_ref, high_ref, low_ref):
    pieces, rows, width = block_ref.shape
    flat = block_ref[...].reshape(pieces * rows, width)
    out = mm(flat, high_ref[...]) + mm(flat, low_ref[...])
    return out.reshape(pieces, rows, 2 * width)


def nyquist_split(spec):
    half = spec.shape[-1] // 2
    real, imaginary = spec[..., :half], spec[..., half:]
    first = lane_of(real.shape) == 0
    return jnp.where(first, 0.0, imaginary), jnp.where(first, imaginary, real)


def norm_body(tok_ref, halo_ref, gains_ref, norm_ref, halo_out):
    gain = gains_ref[0:1, :]
    norm_ref[...] = (normalize_rows(tok_ref[...].astype(F32))[0] * gain).astype(BF16)
    halo_out[...] = (normalize_rows(halo_ref[...].astype(F32))[0] * gain).astype(BF16)


def filter_body(
    lift_ref, map_ref, read_ref, damp_ref, feat_ref, table_ref, s1, c1, s2, c2, spec_ref
):
    sine_one, cosine_one = sincos(mm(lift_ref[...], feat_ref[...], TN, HIGHEST))
    s1[...] = sine_one
    c1[...] = cosine_one
    sine_two, cosine_two = sincos(mm(map_ref[...], sine_one, TN, HIGHEST))
    s2[...] = sine_two
    c2[...] = cosine_two
    shape = (read_ref.shape[1], sine_two.shape[1])
    place = lane_of(shape).astype(F32)
    response = mm(read_ref[...], sine_two, TN, HIGHEST) * jnp.exp(-place * damp_ref[...])
    pieces, span, doubled = spec_ref.shape
    width = doubled // 2
    zero = jnp.zeros((span, width), F32)
    rows = []
    for k in range(pieces):
        now = response[:, k * width : (k + 1) * width]
        before = response[:, (k - 1) * width : k * width] if k else zero
        rows.append(
            jnp.concatenate([now, jnp.where(lane_of(before.shape) == 0, 0.0, before)], 1)
        )
    spec = mm(jnp.concatenate(rows, 0), table_ref[...], NN, HIGHEST)
    spec_ref[...] = spec.reshape(pieces, span, doubled)


def value_body(fast, *refs):
    if fast:
        me_ref, own_ref, other_ref, norm_ref, perm_ref, full_ref, out_ref, gather = refs
        rows = own_ref.shape[1]
        me = me_ref[0]
        for core, held in enumerate((own_ref, other_ref)):
            for r in range(held.shape[0]):
                distance = 2 * core + (0, 4, 1, 5)[r // 4] + 2 * ROUND_Z[r % 4]
                owner = jnp.bitwise_xor(me, distance)
                gather[pl.ds(pl.multiple_of(owner * rows, 8), rows), :] = held[r].astype(F32)
        full_ref[...] = gather[...].astype(BF16)
    else:
        inner_ref, norm_ref, perm_ref, full_ref, out_ref = refs
        full_ref[...] = inner_ref[...]
    width = full_ref.shape[1]
    norm = parts_of(norm_ref[...])
    first = [
        mm(norm[a], full_ref[a * width : (a + 1) * width, :]).astype(BF16) for a in range(BLOCKS)
    ]
    send_pieces(first, perm_ref, out_ref)


def send_pieces(parts, perm_ref, out_ref):
    pieces, rows, width = out_ref.shape
    seqs = parts[0].shape[0] // width
    span = rows // seqs
    turned = [
        sum(
            mm(perm_ref[k], parts[k][s * width : (s + 1) * width], NT) for k in range(BLOCKS)
        )
        for s in range(seqs)
    ]
    for n in range(pieces):
        out_ref[n] = jnp.concatenate(
            [turned[s][n * span : (n + 1) * span] for s in range(seqs)], 0
        ).astype(BF16)


def receive_pieces(in_ref, perm_ref):
    pieces, rows, width = in_ref.shape
    seqs = rows * pieces // (BLOCKS * perm_ref.shape[2])
    span = rows // seqs
    held = [in_ref[n].astype(F32) for n in range(pieces)]
    turned = [
        jnp.concatenate([h[s * span : (s + 1) * span] for h in held], 0).T.astype(BF16)
        for s in range(seqs)
    ]
    return [
        jnp.concatenate([mm(turned[s], perm_ref[k]) for s in range(seqs)], 0)
        for k in range(BLOCKS)
    ]


def earlier_rows(values, halo, steps):
    moved = pltpu.roll(values, steps, 0)
    row = row_of(values.shape)
    for k in range(steps):
        moved = jnp.where(row == k, halo[2 - steps + k : 3 - steps + k], moved)
    return moved


def later_rows(values, halo, steps):
    count = values.shape[0]
    moved = pltpu.roll(values, count - steps, 0)
    row = row_of(values.shape)
    for k in range(steps):
        moved = jnp.where(row == count - steps + k, halo[k : k + 1], moved)
    return moved


def per_sequence(function, values, halo, seqs, steps):
    count = values.shape[0] // seqs
    return jnp.concatenate(
        [
            function(values[s * count : (s + 1) * count], halo[2 * s : 2 * s + 2], steps)
            for s in range(seqs)
        ],
        0,
    )


def switch_body(seqs, norm_ref, halo_ref, full_ref, tw_ref, taps_ref, sect_ref, sw_ref, sh_ref, gate_ref):
    width = norm_ref.shape[1] // BLOCKS
    norm, halo = parts_of(norm_ref[...]), parts_of(halo_ref[...])
    inner = [full_ref[a * width : (a + 1) * width, :][:, :width] for a in range(BLOCKS)]
    first = [mm(norm[a], inner[a]) for a in range(BLOCKS)]
    for a in range(BLOCKS):
        sect_ref[a] = first[a]
    rows = tw_ref[...]
    switch = mix(first, rows)
    edge = mix([mm(halo[a], inner[a]) for a in range(BLOCKS)], rows)
    for b in range(BLOCKS):
        sw_ref[b] = switch[b].astype(BF16)
        sh_ref[b] = edge[b].astype(BF16)
        now = switch[b].astype(BF16).astype(F32)
        before = edge[b].astype(BF16).astype(F32)
        taps = taps_ref[b]
        gate_ref[b] = (
            taps[0:1] * now
            + taps[1:2] * per_sequence(earlier_rows, now, before, seqs, 1)
            + taps[2:3] * per_sequence(earlier_rows, now, before, seqs, 2)
        )


def convolve(spec_ref, b_ref, c_ref, x_ref, y_ref):
    pieces, rows, doubled = x_ref.shape
    span = spec_ref.shape[1]
    half = doubled // 2
    zero = jnp.zeros((span, half), F32)
    seqs = rows // span

    def outer(i, carry):
        def inner(j, totals):
            k = i - j
            a_now, b_now, c_now = spec_ref[k, :, :half], b_ref[k], c_ref[k]
            out = []
            for s in range(seqs):
                real = x_ref[j, s * span : (s + 1) * span, :half]
                imag = x_ref[j, s * span : (s + 1) * span, half:]
                out.append(totals[2 * s] + a_now * real - b_now * imag)
                out.append(totals[2 * s + 1] + b_now * real + c_now * imag)
            return tuple(out)

        totals = lax.fori_loop(0, i + 1, inner, (zero,) * (2 * seqs))
        for s in range(seqs):
            y_ref[i, s * span : (s + 1) * span, :half] = totals[2 * s]
            y_ref[i, s * span : (s + 1) * span, half:] = totals[2 * s + 1]
        return carry

    lax.fori_loop(0, pieces, outer, 0)


def correlate(spec_ref, b_ref, c_ref, g_ref, y_ref):
    pieces, rows, doubled = g_ref.shape
    span = spec_ref.shape[1]
    half = doubled // 2
    zero = jnp.zeros((span, half), F32)
    seqs = rows // span

    def outer(j, carry):
        def inner(i, totals):
            k = i - j
            a_now, b_now, c_now = spec_ref[k, :, :half], b_ref[k], c_ref[k]
            out = []
            for s in range(seqs):
                real = g_ref[i, s * span : (s + 1) * span, :half]
                imag = g_ref[i, s * span : (s + 1) * span, half:]
                out.append(totals[2 * s] + a_now * real + b_now * imag)
                out.append(totals[2 * s + 1] + c_now * imag - b_now * real)
            return tuple(out)

        totals = lax.fori_loop(j, pieces, inner, (zero,) * (2 * seqs))
        for s in range(seqs):
            y_ref[j, s * span : (s + 1) * span, :half] = totals[2 * s]
            y_ref[j, s * span : (s + 1) * span, half:] = totals[2 * s + 1]
        return carry

    lax.fori_loop(0, pieces, outer, 0)


def conv_body(
    length, sect_ref, mix_ref, taps_ref, spec_ref, high_ref, low_ref, back_ref,
    out_ref, cin_ref, signal_ref, x_ref, y_ref, b_ref, c_ref,
):
    span = spec_ref.shape[1]
    lanes_now = time_rows(sect_ref, span).astype(BF16)
    signal = mm(mix_ref[...], lanes_now).astype(BF16)
    signal_ref[...] = signal
    signal = signal.astype(F32)
    conv_in = (
        taps_ref[:, 0:1] * signal
        + taps_ref[:, 1:2] * earlier_lanes(signal, 1, length)
        + taps_ref[:, 2:3] * earlier_lanes(signal, 2, length)
    )
    to_blocks(conv_in, cin_ref, length)
    x_ref[...] = spectrum(cin_ref, high_ref, low_ref)
    b_ref[...], c_ref[...] = nyquist_split(spec_ref[...])
    convolve(spec_ref, b_ref, c_ref, x_ref, y_ref)
    pieces, rows, doubled = y_ref.shape
    out = mm(y_ref[...].reshape(pieces * rows, doubled), back_ref[...], NN, HIGHEST)
    out_ref[...] = out.astype(BF16).reshape(pieces, rows, doubled // 2)


def middle_body(
    seqs, long_ref, gate_ref, tok_ref, cot_ref, gains_ref, full_ref, tw_ref, sp_ref, sq_ref, perm_ref,
    layer_ref, lg_ref, swg_ref, res_ref, hid_ref, n2_ref, gated_ref, fgate_ref, fup_ref,
    fdown_ref, fmerge_ref, spg_ref, sqg_ref, twg_ref, gain_ref, fg, fu, act, ug, hg,
):
    rows, total = tok_ref.shape
    width = total // BLOCKS
    wide = fg.shape[2]
    base = 2 * wide
    gate = [gate_ref[b] for b in range(BLOCKS)]
    long_out = receive_pieces(long_ref, perm_ref)
    gated = [(gate[b] * long_out[b]).astype(BF16) for b in range(BLOCKS)]
    for b in range(BLOCKS):
        gated_ref[b] = gated[b]
    at = [slice(a * width, (a + 1) * width) for a in range(BLOCKS)]
    merge = [full_ref[at[a], 3 * wide :][:, width:] for a in range(BLOCKS)]
    sect_merge = [mm(gated[a], merge[a]) for a in range(BLOCKS)]
    merged = mix(sect_merge, tw_ref[...])
    tokens = parts_of(tok_ref[...].astype(F32))
    residual = [tokens[b] + merged[b] for b in range(BLOCKS)]
    mean = sum(jnp.sum(r, -1, keepdims=True) for r in residual) / total
    centred = [r - mean for r in residual]
    variance = sum(jnp.sum(c * c, -1, keepdims=True) for c in centred) / total
    factor = lax.rsqrt(variance + 1e-05)
    normed = [c * factor for c in centred]
    gain = parts_of(gains_ref[1:2, :])
    for a in range(BLOCKS):
        n2_now = (normed[a] * gain[a]).astype(BF16)
        n2_ref[a] = n2_now
        fg[a] = mm(n2_now, full_ref[at[a], :wide])
        fu[a] = mm(n2_now, full_ref[at[a], wide : 2 * wide])

    step = 16
    lanes = 128

    def forward_chunk(l, r):
        here = pl.ds(pl.multiple_of(l * lanes, lanes), lanes)
        down = pl.ds(pl.multiple_of(r * step, step), step)
        g_rows, u_rows = sp_ref[0, :, here], sp_ref[1, :, here]
        gate_pre = mix([fg[a, down, here] for a in range(BLOCKS)], g_rows)
        up_pre = mix([fu[a, down, here] for a in range(BLOCKS)], u_rows)
        for b in range(BLOCKS):
            v, u = gate_pre[b], up_pre[b]
            square = v * v
            bent = jnp.tanh(0.7978845608 * v * (1.0 + 0.044715 * square))
            half = 0.5 + 0.5 * bent
            active = v * half
            slope = half + 0.5 * v * (1.0 - bent * bent) * (
                0.7978845608 + (3 * 0.044715 * 0.7978845608) * square
            )
            hid_ref[b, down, here] = (active * u).astype(BF16)
            act[b, down, here] = active
            ug[b, down, here] = u * slope

    def forward_lane(l, carry):
        def forward_row(r, inner_carry):
            forward_chunk(l, r)
            return inner_carry

        return lax.fori_loop(0, rows // step, forward_row, carry)

    lax.fori_loop(0, wide // lanes, forward_lane, 0)

    shrink = []
    for a in range(BLOCKS):
        held = full_ref[at[a], base : base + wide]
        shrink.append(jnp.concatenate(parts_of(held), 0))
    sect_down = [mm(hid_ref[a], shrink[a]) for a in range(BLOCKS)]
    lowered = mix(sect_down, sq_ref[...])
    layer_ref[...] = jnp.concatenate(
        [(residual[b] + lowered[b]).astype(BF16) for b in range(BLOCKS)], 1
    )
    upstream = parts_of(cot_ref[...].astype(F32))
    sqg_ref[...] = mix_grad(sect_down, upstream)
    back_down = unmix(upstream, sq_ref[...])
    for a in range(BLOCKS):
        now = back_down[a].astype(BF16)
        fdown_ref[a] = now
        hg[a] = mm(now, shrink[a], NT)

    def backward_lane(l, carry):
        here = pl.ds(pl.multiple_of(l * lanes, lanes), lanes)
        g_rows, u_rows = sp_ref[0, :, here], sp_ref[1, :, here]

        def backward_row(r, sums):
            down = pl.ds(pl.multiple_of(r * step, step), step)
            hidden = [hg[b, down, here] for b in range(BLOCKS)]
            gate_grad = [hidden[b] * ug[b, down, here] for b in range(BLOCKS)]
            up_grad = [hidden[b] * act[b, down, here] for b in range(BLOCKS)]
            for a, value in enumerate(unmix(gate_grad, g_rows)):
                fgate_ref[a, down, here] = value.astype(BF16)
            for a, value in enumerate(unmix(up_grad, u_rows)):
                fup_ref[a, down, here] = value.astype(BF16)
            out = []
            for held, grads, start in ((fg, gate_grad, 0), (fu, up_grad, 16)):
                for a in range(BLOCKS):
                    value = held[a, down, here]
                    for b in range(BLOCKS):
                        product = value * grads[b]
                        out.append(sums[start + 4 * a + b] + product[:8] + product[8:])
            return tuple(out)

        zero = jnp.zeros((8, lanes), F32)
        sums = lax.fori_loop(0, rows // step, backward_row, (zero,) * 32)
        for k in range(32):
            spg_ref[k // 16, pl.ds(k % 16, 1), here] = jnp.sum(sums[k], 0, keepdims=True)
        return carry

    lax.fori_loop(0, wide // lanes, backward_lane, 0)

    n2_grad = [
        mm(fgate_ref[a], full_ref[at[a], :wide], NT)
        + mm(fup_ref[a], full_ref[at[a], wide : 2 * wide], NT)
        for a in range(BLOCKS)
    ]
    scaled = [n2_grad[a] * gain[a] for a in range(BLOCKS)]
    plain = sum(jnp.sum(v, -1, keepdims=True) for v in scaled) / total
    joint = sum(jnp.sum(scaled[a] * normed[a], -1, keepdims=True) for a in range(BLOCKS)) / total
    res_grad = [
        upstream[a] + factor * (scaled[a] - plain - normed[a] * joint) for a in range(BLOCKS)
    ]
    gain_ref[...] = jnp.concatenate(
        [jnp.sum(n2_grad[a] * normed[a], 0, keepdims=True) for a in range(BLOCKS)], 0
    )
    for a in range(BLOCKS):
        res_ref[a] = res_grad[a]
    twg_ref[...] = mix_grad(sect_merge, res_grad)
    back_merge = [v.astype(BF16) for v in unmix(res_grad, tw_ref[...])]
    long_grad = []
    for a in range(BLOCKS):
        fmerge_ref[a] = back_merge[a]
        gated_grad = mm(back_merge[a], merge[a], NT)
        long_grad.append((gated_grad * gate[a]).astype(BF16))
        swg_ref[a] = (gated_grad * long_out[a]).astype(BF16)
    send_pieces(long_grad, perm_ref, lg_ref)


def switch_back_body(
    seqs, swg_ref, next_ref, sw_ref, sh_ref, sect_ref, full_ref, tw_ref, taps_ref,
    n1_ref, fsw_ref, twg_ref, kg_ref,
):
    width = swg_ref.shape[2]
    back = []
    for b in range(BLOCKS):
        grad = swg_ref[b].astype(F32)
        after = next_ref[b].astype(F32)
        taps = taps_ref[b]
        back.append(
            taps[0:1] * grad
            + taps[1:2] * per_sequence(later_rows, grad, after, seqs, 1)
            + taps[2:3] * per_sequence(later_rows, grad, after, seqs, 2)
        )
        now, before = sw_ref[b].astype(F32), sh_ref[b].astype(F32)
        shifted = [now] + [per_sequence(earlier_rows, now, before, seqs, m) for m in (1, 2)]
        kg_ref[b] = jnp.concatenate(
            [jnp.sum(value * grad, 0, keepdims=True) for value in shifted], 0
        )
    twg_ref[...] = mix_grad([sect_ref[a] for a in range(BLOCKS)], back)
    first = unmix(back, tw_ref[...])
    for a in range(BLOCKS):
        now = first[a].astype(BF16)
        fsw_ref[a] = now
        n1_ref[a] = mm(now, full_ref[a * width : (a + 1) * width, :][:, :width], NT)


def weight_grad_body(
    fast, me_ref, n2_ref, fgate_ref, fup_ref, hid_ref, fdown_ref, gated_ref, fmerge_ref,
    norm_ref, fsw_ref, small_ref, *outs,
):
    norm = parts_of(norm_ref[...])
    count, rows, _ = small_ref.shape
    share = count // BLOCKS
    width = n2_ref.shape[2]
    for a in range(BLOCKS):
        shrink = mm(hid_ref[a], fdown_ref[a], TN)
        held = jnp.concatenate(
            [mm(n2_ref[a], fgate_ref[a], TN), mm(n2_ref[a], fup_ref[a], TN)]
            + [shrink[g * width : (g + 1) * width] for g in range(BLOCKS)]
            + [mm(norm[a], fsw_ref[a], TN), mm(gated_ref[a], fmerge_ref[a], TN)],
            1,
        )
        if not fast:
            outs[0][a * width : (a + 1) * width, :] = held
            continue
        half = outs[0].shape[2]
        for k in range(share):
            owner = a * share + k
            block = held[k * rows : (k + 1) * rows]
            apart = jnp.bitwise_xor(me_ref[0], owner)
            bits = [jnp.bitwise_and(lax.shift_right_logical(apart, n), 1) for n in range(5)]
            left = bits[1] * 16 + bits[0] * 8 + bits[2] * 4 + bits[3] * 2 + bits[4]
            right = bits[1] * 16 + bits[2] * 8 + bits[0] * 4 + bits[3] * 2 + bits[4]
            outs[0][left] = block[:, :half].astype(BF16)
            outs[1][right] = jnp.concatenate([block[:, half:], small_ref[owner]], 1).astype(BF16)


def conv_back_body(
    length, g_ref, mix_ref, taps_ref, spec_ref, high_ref, low_ref, back_ref,
    out_ref, cg_ref, sg_ref, x_ref, y_ref, b_ref, c_ref,
):
    span = spec_ref.shape[1]
    x_ref[...] = spectrum(g_ref, high_ref, low_ref)
    b_ref[...], c_ref[...] = nyquist_split(spec_ref[...])
    correlate(spec_ref, b_ref, c_ref, x_ref, y_ref)
    pieces, rows, doubled = y_ref.shape
    flat = mm(y_ref[...].reshape(pieces * rows, doubled), back_ref[...], NN, HIGHEST)
    flat = flat.astype(BF16).astype(F32)
    grad = jnp.concatenate(
        [
            flat[n * rows + s * span : n * rows + (s + 1) * span]
            for s in range(rows // span)
            for n in range(pieces)
        ],
        1,
    )
    cg_ref[...] = grad.astype(BF16)
    signal_grad = (
        taps_ref[:, 0:1] * grad
        + taps_ref[:, 1:2] * later_lanes(grad, 1, length)
        + taps_ref[:, 2:3] * later_lanes(grad, 2, length)
    )
    sg_ref[...] = signal_grad
    to_blocks(mm(mix_ref[...].astype(F32), signal_grad, TN, HIGHEST), out_ref, length)


def filter_back_body(
    length, g_ref, cin_ref, sect_ref, signal_ref, cg_ref, sg_ref, s1, c1, s2, c2, read_ref, map_ref,
    damp_ref, feat_ref, high_ref, low_ref, back_ref, same_ref, pick_ref,
    m_ref, q_ref, x_ref, b_ref, c_ref, gs_ref, p_ref,
):
    pieces, span, doubled = p_ref.shape
    half = doubled // 2
    x_ref[...] = spectrum(cin_ref, high_ref, low_ref)
    b_ref[...], c_ref[...] = nyquist_split(x_ref[...])
    gs_ref[...] = spectrum(g_ref, high_ref, low_ref)
    seqs = x_ref.shape[1] // span
    zero = jnp.zeros((span, half), F32)

    def outer(k, carry):
        def inner(j, totals):
            real, imag = totals
            for s in range(seqs):
                at = slice(s * span, (s + 1) * span)
                a_now, b_now, c_now = x_ref[j, at, :half], b_ref[j, at], c_ref[j, at]
                g_real, g_imag = gs_ref[j + k, at, :half], gs_ref[j + k, at, half:]
                real = real + a_now * g_real + b_now * g_imag
                imag = imag + c_now * g_imag - b_now * g_real
            return real, imag

        real, imag = lax.fori_loop(0, pieces - k, inner, (zero, zero))
        p_ref[k, :, :half] = real
        p_ref[k, :, half:] = imag
        return carry

    lax.fori_loop(0, pieces, outer, 0)
    flat = mm(p_ref[...].reshape(pieces * span, doubled), back_ref[...], NN, HIGHEST)
    chunks = []
    for k in range(pieces):
        now = flat[k * span : (k + 1) * span, :half]
        if k + 1 < pieces:
            after = flat[(k + 1) * span : (k + 2) * span, half:]
            now = now + jnp.where(lane_of(after.shape) == 0, 0.0, after)
        chunks.append(now)
    response_grad = jnp.concatenate(chunks, 1)
    place = lane_of(response_grad.shape).astype(F32)
    response_grad = response_grad * jnp.exp(-place * damp_ref[...])
    readout_grad = mm(response_grad, s2[...], NT, HIGHEST)
    pre_two = mm(read_ref[...], response_grad, NN, HIGHEST) * c2[...]
    order = s1.shape[0]
    m_ref[:order, :] = mm(s1[...], pre_two, NT, HIGHEST)
    pre_one = mm(map_ref[...], pre_two, NN, HIGHEST) * c1[...]
    m_ref[order:, :] = mm(feat_ref[...], pre_one, NT, HIGHEST)

    sect = time_rows(sect_ref, span)
    tw = mm(sect, sg_ref[...], NT, HIGHEST) * same_ref[...]
    tw = mm(pick_ref[...], tw, NN, HIGHEST)
    cg = cg_ref[...].astype(F32)
    signal = signal_ref[...].astype(F32)
    ones = jnp.ones((8, cg.shape[1]), F32)
    row = row_of(tw.shape)
    for m in range(3):
        moved = signal if m == 0 else earlier_lanes(signal, m, length)
        tw = jnp.where(row == BLOCKS + m, mm(ones, moved * cg, NT, HIGHEST), tw)
    q_ref[:span, :] = readout_grad
    q_ref[span:, :] = jnp.concatenate([tw, jnp.zeros((8, q_ref.shape[1] - span), F32)], 1)


def last_body(
    fast, fg_ref, perm_ref, inner_ref, norm_ref, n1_ref, res_ref, tok_ref, gains_ref, out_ref, *pay
):
    width = inner_ref.shape[1]
    first = [v.astype(BF16) for v in receive_pieces(fg_ref, perm_ref)]
    norm = parts_of(norm_ref[...])
    normed, factor = normalize_rows(tok_ref[...].astype(F32))
    normed = parts_of(normed)
    gain = parts_of(gains_ref[0:1, :])
    grads = [
        mm(first[a], inner_ref[a * width : (a + 1) * width, :], NT) + n1_ref[a]
        for a in range(BLOCKS)
    ]
    scaled = [grads[a] * gain[a] for a in range(BLOCKS)]
    total = width * BLOCKS
    plain = sum(jnp.sum(v, -1, keepdims=True) for v in scaled) / total
    joint = sum(jnp.sum(scaled[a] * normed[a], -1, keepdims=True) for a in range(BLOCKS)) / total
    out_ref[...] = jnp.concatenate(
        [res_ref[a] + factor * (scaled[a] - plain - normed[a] * joint) for a in range(BLOCKS)], 1
    )
    gain_grad = [jnp.sum(grads[a] * normed[a], 0, keepdims=True) for a in range(BLOCKS)]
    weight = [mm(norm[a], first[a], TN) for a in range(BLOCKS)]
    if not fast:
        for a in range(BLOCKS):
            pay[0][a * width : (a + 1) * width, :] = weight[a]
            pay[1][a : a + 1, :] = gain_grad[a]
        return
    count, rows, _ = pay[0].shape
    share = count // BLOCKS
    held = rows - 8
    tail = jnp.concatenate(gain_grad + [jnp.zeros((4, width), F32)], 0)
    for a in range(BLOCKS):
        for k in range(share):
            block = weight[a][k * held : (k + 1) * held]
            pay[0][a * share + k] = jnp.concatenate([block, tail], 0).astype(BF16)


def hop(values, distance):
    pieces = lax.axis_size("seq")
    return lax.ppermute(values, "seq", [(n, n ^ distance) for n in range(pieces)])


def hop_y(values):
    return lax.ppermute(values, "batch", [(0, 1), (1, 0)])


def hop_xy(values):
    return lax.ppermute(values, BOTH, [(n, n ^ 5) for n in range(2 * lax.axis_size("seq"))])


def per_device(
    tokens,
    cotangent,
    gains,
    mixing,
    twiddle,
    expand,
    spread,
    shrink,
    squeeze,
    kernel,
    lifting,
    phases,
    mapping,
    readout,
    damping,
):
    seqs, share, total = tokens.shape
    pieces, groups = lax.axis_size("seq"), lax.axis_size("batch")
    devices = pieces * groups
    place = lax.axis_index("seq")
    me = (place * groups + lax.axis_index("batch")).astype(jnp.int32).reshape(1)
    rows = seqs * share
    length = pieces * share
    width = total // BLOCKS
    wide = expand.shape[2]
    span = width // pieces
    chans = BLOCKS * span
    owned = mixing.shape[1]
    octet = devices // BLOCKS
    order = mapping.shape[0]
    fast = pieces == 16 and groups == 2 and owned % 8 == 0

    table, table_back = packed_tables(share)
    high, low = split_table(table[:share])
    perm = spread_matrix(pieces, span)
    feats = feature_rows(length)
    same = np.tile(np.eye(span, dtype=np.float32), (BLOCKS, BLOCKS))
    pick = np.zeros((8, chans), np.float32)
    for a in range(BLOCKS):
        pick[a, a * span : (a + 1) * span] = 1.0

    if fast:
        held = jnp.stack([mixing[0]] + [hop(mixing[0], d) for d in ROUND_Z[1:]])
        held = jnp.concatenate([held, hop(held, 2), hop_y(held), hop_xy(held)], 0)
        inner_parts = (held, hop(held, 1))
    else:
        inner_parts = (lax.all_gather(mixing[0], BOTH, axis=0, tiled=True),)
    expand_own = expand.reshape(2, owned, octet, BLOCKS, owned).swapaxes(2, 3)
    expand_own = expand_own.reshape(2, owned, wide)
    shrink_own = shrink.reshape(BLOCKS, owned, width).swapaxes(0, 1).reshape(owned, BLOCKS * width)
    packed = jnp.concatenate(
        [expand_own[0], expand_own[1], shrink_own, mixing[1], mixing[2]], 1
    )
    full = lax.all_gather(packed, BOTH, axis=0, tiled=True)
    pair = full[:, 3 * wide :]

    tok = tokens.reshape(rows, total)
    cot = cotangent.reshape(rows, total)
    halo = lax.ppermute(
        tokens[:, share - 2 :], "seq", [(n, n + 1) for n in range(pieces - 1)]
    ).reshape(2 * seqs, total)
    halo = jnp.pad(halo, ((0, 16 - 2 * seqs), (0, 0)))
    norm, norm_halo = call(norm_body, [((rows, total), BF16), ((16, total), BF16)], [tok, halo, gains])

    lift = jnp.concatenate([lifting, phases[None], jnp.zeros((2, order), F32)], 0)
    own_cols = jnp.concatenate([readout, damping[None], kernel[:, :total]], 0)
    own_cols = own_cols.reshape(order + 4, BLOCKS, pieces, span)
    own_cols = lax.dynamic_index_in_dim(own_cols, place, 2, False).reshape(order + 4, chans)
    read_own = own_cols[:order]
    turned = own_cols[order:].T
    damp_own, taps_own = turned[:, :1], turned[:, 1:]
    s1, c1, s2, c2, spec = call(
        filter_body,
        [((order, length), F32)] * 4 + [((pieces, chans, 2 * share), F32)],
        [lift, mapping, read_own, damp_own, feats, table],
        flops=5e9,
    )
    tw_rows = twiddle.astype(F32).transpose(0, 2, 3, 1).reshape(3, 16, width)
    sq_rows = squeeze.astype(F32).transpose(1, 2, 0).reshape(16, width)
    sp_rows = spread.astype(F32).reshape(2, octet, BLOCKS, owned, 16)
    sp_rows = sp_rows.transpose(0, 4, 2, 1, 3).reshape(2, 16, wide)
    tw_own = lax.dynamic_slice_in_dim(twiddle[0], place * span, span, 0)
    mix_own = jnp.einsum("jab,jk->bjak", tw_own, jnp.eye(span, dtype=BF16)).reshape(chans, chans)
    taps_sw = kernel[:, total:].reshape(3, BLOCKS, width).swapaxes(0, 1)

    blocks = (pieces, seqs * chans, share)
    inner, sect_out = call(
        functools.partial(value_body, fast),
        [((total, width), BF16), (blocks, BF16)],
        ([me] if fast else []) + list(inner_parts) + [norm, perm],
        scratch=[pltpu.VMEM((total, width), F32)] if fast else [],
        scalars=1 if fast else 0,
        flops=1e9,
    )
    sect_in = lax.all_to_all(sect_out, "seq", 0, 0, tiled=True)
    spectra = (pieces, seqs * chans, 2 * share)
    conv_scratch = [
        pltpu.VMEM(spectra, F32),
        pltpu.VMEM(spectra, F32),
        pltpu.VMEM((pieces, chans, share), F32),
        pltpu.VMEM((pieces, chans, share), F32),
    ]
    long_out, conv_in, signal = call(
        functools.partial(conv_body, length),
        [(blocks, BF16), (blocks, BF16), ((chans, seqs * length), BF16)],
        [sect_in, mix_own, taps_own, spec, high, low, table_back[:, :share]],
        scratch=conv_scratch,
        flops=3e9,
    )
    long_in = lax.all_to_all(long_out, "seq", 0, 0, tiled=True)

    quad = (BLOCKS, rows, width)
    sect_sw, switch, switch_edge, gate_seq = call(
        functools.partial(switch_body, seqs),
        [(quad, F32), (quad, BF16), ((BLOCKS, 16, width), BF16), (quad, F32)],
        [norm, norm_halo, pair, tw_rows[1], taps_sw],
        flops=2e9,
    )

    broad = (BLOCKS, rows, wide)
    (
        layer, lg_out, switch_grad, res_grad, hidden, norm_two, gated, fgate, fup, fdown, fmerge,
        spread_part, squeeze_part, merge_part, gain_part,
    ) = call(
        functools.partial(middle_body, seqs),
        [
            ((rows, total), BF16), (blocks, BF16), (quad, BF16), (quad, F32), (broad, BF16),
            (quad, BF16), (quad, BF16), (broad, BF16), (broad, BF16), (quad, BF16), (quad, BF16),
            ((2, 16, wide), F32), ((16, width), F32), ((16, width), F32), ((BLOCKS, width), F32),
        ],
        [long_in, gate_seq, tok, cot, gains, full, tw_rows[2], sp_rows, sq_rows, perm],
        scratch=[pltpu.VMEM(broad, F32)] * 5,
        limit=56,
        flops=2e10,
    )
    lg_in = lax.all_to_all(lg_out, "seq", 0, 0, tiled=True)

    first_rows = switch_grad.reshape(BLOCKS, seqs, share, width)[:, :, :2]
    after = lax.ppermute(first_rows, "seq", [(n + 1, n) for n in range(pieces - 1)])
    after = after.reshape(BLOCKS, 2 * seqs, width)
    n1_sw, fsw, switch_part, taps_part = call(
        functools.partial(switch_back_body, seqs),
        [(quad, F32), (quad, BF16), ((16, width), F32), ((BLOCKS, 3, width), F32)],
        [switch_grad, after, switch, switch_edge, sect_sw, pair, tw_rows[1], taps_sw],
        flops=2e9,
    )

    small_parts = (spread_part, squeeze_part, merge_part, switch_part, gain_part, taps_part)
    small_sizes = [p.size for p in small_parts]
    small = jnp.concatenate([p.reshape(-1) for p in small_parts])
    lot = 128 * devices
    each = -(-small.size // lot)
    packed_width = 3 * wide + 2 * width
    small = jnp.pad(small, (0, each * lot - small.size)).reshape(devices, each, 128)
    small_rows = jnp.pad(small, ((0, 0), (0, max(owned - each, 0)), (0, 0)))[:, :owned]
    if fast:
        half = (packed_width + 128) // 2
        grad_shapes = [((devices, owned, half), BF16)] * 2
    else:
        grad_shapes = [((total, packed_width), F32)]
    grads = call(
        functools.partial(weight_grad_body, fast),
        grad_shapes,
        [me, norm_two, fgate, fup, hidden, fdown, gated, fmerge, norm, fsw, small_rows],
        scalars=1,
        flops=1e10,
    )
    if fast:
        left, right = grads
        orders = ((1, 1), ("y", 2), (2, "y"), (4, 4), (8, 8))
        left, right = left.astype(BF16), right.astype(BF16)
        for k, (d_left, d_right) in enumerate(orders):
            n = left.shape[0] // 2
            kind = F32 if k == len(orders) - 1 else BF16
            pair_now = []
            for value, d in ((left, d_left), (right, d_right)):
                sent = hop_y(value[n:]) if d == "y" else hop(value[n:], d)
                pair_now.append((value[:n].astype(F32) + sent.astype(F32)).astype(kind))
            left, right = pair_now
        owner_grads = jnp.concatenate([left[0], right[0]], 1)
    else:
        owner_grads = lax.psum_scatter(grads[0], BOTH, scatter_dimension=0, tiled=True)

    fg_out, conv_grad, signal_grad = call(
        functools.partial(conv_back_body, length),
        [(blocks, BF16), ((chans, seqs * length), BF16), ((chans, seqs * length), F32)],
        [lg_in, mix_own, taps_own, spec, high, low, table_back[:, :share]],
        scratch=conv_scratch,
        flops=3e9,
    )
    fg_in = lax.all_to_all(fg_out, "seq", 0, 0, tiled=True)

    q_rows = chans + 8
    m_part, q_part = call(
        functools.partial(filter_back_body, length),
        [((order + 8, order), F32), ((q_rows, order), F32)],
        [
            lg_in, conv_in, sect_in, signal, conv_grad, signal_grad, s1, c1, s2, c2, read_own,
            mapping, damp_own, feats, high, low, table_back, same, pick,
        ],
        scratch=[
            pltpu.VMEM(spectra, F32),
            pltpu.VMEM(blocks, F32),
            pltpu.VMEM(blocks, F32),
            pltpu.VMEM(spectra, F32),
            pltpu.VMEM((pieces, chans, 2 * share), F32),
        ],
        flops=5e9,
    )

    if fast:
        last_shapes = [((devices, owned + 8, width), BF16)]
    else:
        last_shapes = [((total, width), F32), ((BLOCKS, width), F32)]
    tokens_grad, *pay = call(
        functools.partial(last_body, fast),
        [((rows, total), F32)] + last_shapes,
        [fg_in, perm, inner, norm, n1_sw, res_grad, tok, gains],
        flops=2e9,
    )
    if fast:
        value_sum = jnp.sum(lax.all_to_all(pay[0], BOTH, 0, 0, tiled=True).astype(F32), 0)
        value_grad, gain_one = value_sum[:owned], value_sum[owned : owned + BLOCKS]
    else:
        value_grad = lax.psum_scatter(pay[0], BOTH, scatter_dimension=0, tiled=True)
        gain_one = lax.psum(pay[1], BOTH)

    if fast:
        small_own = owner_grads[:each, packed_width:]
        m_rows, part_rows = order + 8, order + 8 + q_rows
        both = jnp.concatenate([m_part, q_part, small_own], 0)
        came = hop_y(both)
        both_mq = both[:part_rows] + came[:part_rows]
        m_sum = both_mq[:m_rows]
        rest = jnp.concatenate([both_mq[m_rows:], small_own, came[part_rows:]], 0)
        got = [hop(jnp.concatenate([m_sum, rest], 0), d) for d in ROUND_Z[1:]]
        m_sum = m_sum + sum(g[:m_rows] for g in got)
        rest = jnp.concatenate([rest] + [g[m_rows:] for g in got], 0)
        sent = jnp.concatenate([m_sum, rest], 0)
        got = [hop(sent, d) for d in ROUND_XC[1:]]
        m_sum = m_sum + sum(g[:m_rows] for g in got)
        rest = jnp.stack([rest] + [g[m_rows:] for g in got])
        rest = rest.reshape(pieces, -1, order)
        where_of = np.zeros(pieces, np.int32)
        for n, outer_d in enumerate(ROUND_XC):
            for k, inner_d in enumerate(ROUND_Z):
                where_of[outer_d ^ inner_d] = 4 * n + k
        index = jnp.asarray(where_of)[jnp.bitwise_xor(jnp.arange(pieces, dtype=jnp.int32), place)]
        rest = jnp.take(rest, index, axis=0)
        q_all = rest[:, :q_rows]
        small_pair = rest[:, q_rows:].reshape(pieces, 2, each, 128)
        mine = lax.axis_index("batch")
        small_pair = jnp.where(mine == 0, small_pair, small_pair[:, ::-1])
        small_all = small_pair.reshape(-1)
    else:
        m_sum = lax.psum(m_part, BOTH)
        q_all = lax.all_gather(lax.psum(q_part, "batch"), "seq", axis=0, tiled=False)
        small_all = lax.psum(small.reshape(-1), BOTH)
    taken, start = [], 0
    for part, size in zip(small_parts, small_sizes):
        taken.append(small_all[start : start + size].reshape(part.shape))
        start += size
    spread_sum, squeeze_sum, merge_sum, switch_sum, gain_two, taps_sum = taken
    spread_grad = spread_sum.reshape(2, 16, BLOCKS, octet, owned).transpose(0, 3, 2, 4, 1)
    spread_grad = spread_grad.reshape(2, wide, BLOCKS, BLOCKS)
    squeeze_grad = squeeze_sum.T.reshape(width, BLOCKS, BLOCKS)
    twiddle_value = q_all[:, chans : chans + BLOCKS, :chans].reshape(pieces, BLOCKS, BLOCKS, span)
    twiddle_value = twiddle_value.transpose(0, 3, 1, 2).reshape(width, BLOCKS, BLOCKS)
    twiddle_grad = jnp.stack(
        [twiddle_value]
        + [v.T.reshape(width, BLOCKS, BLOCKS) for v in (switch_sum, merge_sum)]
    )
    taps_value = q_all[:, chans + BLOCKS : chans + BLOCKS + 3, :chans]
    taps_value = taps_value.reshape(pieces, 3, BLOCKS, span).transpose(1, 2, 0, 3)
    kernel_grad = jnp.concatenate(
        [taps_value.reshape(3, total), taps_sum.swapaxes(0, 1).reshape(3, total)], 1
    )
    readout_grad = q_all[:, :chans].reshape(pieces, BLOCKS, span, order)
    readout_grad = readout_grad.transpose(3, 1, 0, 2).reshape(order, total)
    gains_grad = jnp.stack([gain_one.reshape(total), gain_two.reshape(total)])

    def natural(grad):
        return grad.reshape(owned, BLOCKS, octet, owned).swapaxes(1, 2).reshape(owned, wide)

    expand_grad = jnp.stack(
        [natural(owner_grads[:, :wide]), natural(owner_grads[:, wide : 2 * wide])]
    )
    shrink_grad = owner_grads[:, 2 * wide : 3 * wide].reshape(owned, BLOCKS, width)
    shrink_grad = shrink_grad.swapaxes(0, 1).reshape(BLOCKS * owned, width)
    mixing_grad = jnp.stack(
        [
            value_grad,
            owner_grads[:, 3 * wide : 3 * wide + width],
            owner_grads[:, 3 * wide + width : packed_width],
        ]
    )
    return (
        layer.reshape(seqs, share, total),
        tokens_grad.reshape(seqs, share, total),
        gains_grad,
        mixing_grad,
        twiddle_grad,
        expand_grad,
        spread_grad,
        shrink_grad,
        squeeze_grad,
        kernel_grad,
        m_sum[order : order + lifting.shape[0]],
        m_sum[order + lifting.shape[0]],
        m_sum[:order],
        readout_grad,
    )


def solution(mesh):
    return jax.shard_map(
        per_device,
        mesh=mesh,
        in_specs=(
            P("batch", "seq", None),
            P("batch", "seq", None),
            P(),
            P(None, ("seq", "batch"), None),
            P(),
            P(None, ("seq", "batch"), None),
            P(),
            P(("seq", "batch"), None),
            P(),
            P(),
            P(),
            P(),
            P(),
            P(),
            P(),
        ),
        out_specs=(
            P("batch", "seq", None),
            P("batch", "seq", None),
            P(),
            P(None, ("seq", "batch"), None),
            P(),
            P(None, ("seq", "batch"), None),
            P(),
            P(("seq", "batch"), None),
            P(),
            P(),
            P(),
            P(),
            P(),
            P(),
        ),
        check_vma=False,
    )
```

time: 1320 us -> 282 us (0.21)
  waiting for transfers between devices: 517 us -> 50.6 us
  matrix products: 338 us -> 0 us
  local copies, waits for them, and re-layouts: 207 us -> 62.7 us
  other arithmetic: 151 us -> 9.75 us
  blocking collectives: 74.1 us -> 0 us
  Pallas kernels: 0 us -> 70.9 us
  starting transfers between devices: 10.2 us -> 66.8 us
    dot_general x57 -> x0, matrix products: 335 us -> none  [the longest x3 68.9 us: transform(): jnp.einsum('fn,smnd->smfd', cos_half, grouped, precision=HIGHEST)]
    reduce_scatter x2 -> x0, waiting for transfers between devices: 217 us -> none  [the longest x1 113 us: per_device(): lax.psum_scatter(expand_grad, ('seq', 'batch'), scatter_dimension=1, tile...]
    psum x2 -> x0, waiting for transfers between devices: 191 us -> none  [per_device(): lax.psum((jnp.stack([gain_one_grad, gain_two_grad]), jnp.stack([twiddle_s...]
    unnamed x10 -> x1, waiting for transfers between devices: 106 us -> 0.02 us
    all_gather x1 -> x0, blocking collectives: 74.1 us -> none  [per_device(): lax.all_gather(mixing, ('seq', 'batch'), axis=1, tiled=True)]
    pallas_call x0 -> x11, Pallas kernels: none -> 70.9 us  [call(): pl.pallas_call(body, out_shape=[jax.ShapeDtypeStruct(shape, kind) for sha...]
    mul x4 -> x0, other arithmetic: 58 us -> none  [the longest x1 19.5 us: per_device(): kern_real[None] * collect_real_part + kern_imag[None] * collect_imaginary]
    scatter-add x2 -> x0, other arithmetic: 57.1 us -> none  [the longest x1 28.6 us: per_device(): resp_real = totals[2].at[lag_index].add(prod_real)]
  transfers between devices with their start and end apart: 13 -> 32, of which waited for: 6 -> 13; matrix products, arithmetic and copies ran while one was open for 22% -> 9% of each run, Pallas kernels for 0% -> 17%
where the time goes in v1:
time: 282 us; the launch traced here: 276 us
  Pallas kernels  70.9 us (25%)
  starting transfers between devices  66.8 us (24%)
  local copies, waits for them, and re-layouts  62.7 us (22%)
  waiting for transfers between devices  50.6 us (18%)
  between operations  15.6 us (6%)
  other arithmetic  9.75 us (3%)
    pallas_call x11, Pallas kernels, call(): pl.pallas_call(body, out_shape=[jax.ShapeDtypeStruct(shape, kind) for sha...  70.9 us
    unnamed x150, local copies, waits for them, and re-layouts  36 us
    ppermute x19, starting transfers between devices, hop(): lax.ppermute(values, 'seq', [(n, n ^ distance) for n in range(pieces)])  27.9 us
    ppermute x19, waiting for transfers between devices, hop(): lax.ppermute(values, 'seq', [(n, n ^ distance) for n in range(pieces)])  19.5 us
    all_gather x1, waiting for transfers between devices, per_device(): full = lax.all_gather(packed, BOTH, axis=0, tiled=True)  11.8 us
    all_to_all x1, starting transfers between devices, per_device(): fg_in = lax.all_to_all(fg_out, 'seq', 0, 0, tiled=True)  9.07 us
    ppermute x4, waiting for transfers between devices, hop_y(): return lax.ppermute(values, 'batch', [(0, 1), (1, 0)])  8.73 us
    convert_element_type x8, other arithmetic, per_device(): pair_now.append((value[:n].astype(F32) + sent.astype(F32)).astype(kind))  5.83 us
  transfers between devices with their start and end apart: 32, of which 13 were waited for; matrix products, arithmetic and copies ran while one was open for 9% of the time, Pallas kernels for 17%

profile of v1, /device:TPU:1, one launch (start us, length us, event | category | flops | bytes accessed | tf_op | source)
XLA Modules:
  0.0 276.3 jit_solution(17817810095643544795)
XLA Ops:
  11.2 2.2 collective-permute-start
  13.4 2.3 collective-permute-start.1
  15.7 4.5 %collective-permute-start.7 = (bf16[2,2,768]{2,1,0:T(2,128)(2,1)S(1)}, bf16[2,2,768]{2,1,0:T(2,128)(2,1)S(1)}, u32[]{:S(2)}, u32[]{:S(2)}) collective-permute-start(bf16[2,2,768]{2,1,0:T(2,128)(2,1)S(1)} %slice.253), channel_id=1, source_target_pairs={{0,2},{2,4},{4,6},{6,8},{8,10},{10,12},{12,14},{14,16},{16,18},{18... | collective-permute-start | bytes 18440 | tf_op jit(solution)/shard_map/ppermute | solution.py:815
  24.4 3.2 %collective-permute-done.5 = bf16[4,24,192]{2,1,0:T(8,128)(2,1)S(1)} collective-permute-done((bf16[4,24,192]{2,1,0:T(8,128)(2,1)S(1)}, bf16[4,24,192]{2,1,0:T(8,128)(2,1)S(1)}, u32[]{:S(2)}, u32[]{:S(2)}) %collective-permute-start.5) | collective-permute-done | bytes 36896 | tf_op jit(solution)/shard_map/ppermute | solution.py:753
  27.6 2.9 %collective-permute-start.6 = (bf16[16,24,192]{2,1,0:T(8,128)(2,1)S(1)}, bf16[16,24,192]{2,1,0:T(8,128)(2,1)S(1)}, u32[]{:S(2)}, u32[]{:S(2)}) collective-permute-start(bf16[16,24,192]{2,1,0:T(8,128)(2,1)S(1)} %constant_dynamic-update-slice_fusion.refs_1_), channel_id=1, source_target_pairs={{0,2},{2,0},{4,6},{6,4},{8,10},{10,8},{12,14},{14,12},{16,18},{18,... | collective-permute-start | bytes 442376 | tf_op jit(solution)/shard_map/ppermute | solution.py:745
  36.4 3.7 %all-to-all-start = ((bf16[16,96,128]{2,1,0:T(8,128)(2,1)}), bf16[16,96,128]{2,1,0:T(8,128)(2,1)S(1)}, u32[]{:S(2)}, u32[]{:S(2)}) async-start(bf16[16,96,128]{2,1,0:T(8,128)(2,1)} %get-tuple-element.59), calls=%async_computation | async-start | bytes 786432 | tf_op jit(solution)/shard_map/all_to_all | solution.py:851
  41.1 4.8 %shard_map.355 = (f32[128,2048]{1,0:T(8,128)S(1)}, f32[128,2048]{1,0:T(8,128)S(1)}, f32[128,2048]{1,0:T(8,128)S(1)}, f32[128,2048]{1,0:T(8,128)S(1)}, f32[16,48,256]{2,1,0:T(8,128)S(1)}) custom-call(f32[8,128]{1,0:T(8,128)S(1)} %maximum_maximum_fusion.lift_ref, f32[128,128]{1,0:T(8,128)S(1)} %copy-done.5, f32[128,48]{1,0:T(8,128)S(1)} %copy.85.read_ref, ...), custom_call_target="tpu_custom_call" | custom-call | flops 5000000000 | bytes 1048576 | tf_op jit(solution)/shard_map/pallas_call | solution.py:35
  50.7 5.1 %all-to-all-done.sect_ref = bf16[16,96,128]{2,1,0:T(8,128)(2,1)S(1)} async-done(((bf16[16,96,128]{2,1,0:T(8,128)(2,1)}), bf16[16,96,128]{2,1,0:T(8,128)(2,1)S(1)}, u32[]{:S(2)}, u32[]{:S(2)}) %all-to-all-start) | async-done | bytes 393248 | tf_op jit(solution)/shard_map/all_to_all | solution.py:851
  57.0 7.1 %shard_map.356 = (bf16[16,96,128]{2,1,0:T(8,128)(2,1)}, bf16[16,96,128]{2,1,0:T(8,128)(2,1)S(1)}, bf16[48,4096]{1,0:T(8,128)(2,1)S(1)}) custom-call(bf16[16,96,128]{2,1,0:T(8,128)(2,1)S(1)} %all-to-all-done.sect_ref, bf16[48,48]{1,0:T(8,128)(2,1)S(1)} %reshape.220.mix_ref, f32[48,3]{1,0:T(8,128)S(1)} %slice.335.taps_ref, f32[16,48,256]{2,1,0:T(8,128)S(1)} %copy-done.35, ...), custom_call_target="tpu_custom_call" | custom-call | flops 3000000000 | bytes 1048576 | tf_op jit(solution)/shard_map/pallas_call | solution.py:35
  64.9 5.3 %all-to-all-start.1 = ((bf16[16,96,128]{2,1,0:T(8,128)(2,1)}), bf16[16,96,128]{2,1,0:T(8,128)(2,1)}, u32[]{:S(2)}, u32[]{:S(2)}) async-start(bf16[16,96,128]{2,1,0:T(8,128)(2,1)} %get-tuple-element.61), calls=%async_computation.1 | async-start | bytes 786432 | tf_op jit(solution)/shard_map/all_to_all | solution.py:866
  74.0 11.8 %all-gather.2.cloned.1.call-done.full_ref = bf16[768,2688]{1,0:T(8,128)(2,1)} async-done(((bf16[24,2688]{1,0:T(8,128)(2,1)}), bf16[768,2688]{1,0:T(8,128)(2,1)}) %all-gather.2.cloned.1.call-update) | async-done | bytes 4128784 | tf_op jit(solution)/shard_map/all_gather | solution.py:810
  90.7 23.3 %shard_map.358 = (bf16[256,768]{1,0:T(8,128)(2,1)}, bf16[16,96,128]{2,1,0:T(8,128)(2,1)}, bf16[4,256,192]{2,1,0:T(8,128)(2,1)}, f32[4,256,192]{2,1,0:T(8,128)}, ...) custom-call(bf16[16,96,128]{2,1,0:T(8,128)(2,1)} %all-to-all-done.1., ...), custom_call_target="tpu_custom_call" | custom-call | flops 20000000000 | bytes 1048576 | tf_op jit(solution)/shard_map/pallas_call | solution.py:35
  114.0 3.7 %all-to-all-start.2 = ((bf16[16,96,128]{2,1,0:T(8,128)(2,1)}), bf16[16,96,128]{2,1,0:T(8,128)(2,1)S(1)}, u32[]{:S(2)}, u32[]{:S(2)}) async-start(bf16[16,96,128]{2,1,0:T(8,128)(2,1)} %get-tuple-element.65), calls=%async_computation.2 | async-start | bytes 786432 | tf_op jit(solution)/shard_map/all_to_all | solution.py:892
  118.9 2.6 collective-permute-start.8
  121.6 2.3 collective-permute-done.8
  135.4 5.5 %shard_map.363 = (bf16[32,24,1408]{2,1,0:T(8,128)(2,1)}, bf16[32,24,1408]{2,1,0:T(8,128)(2,1)}) custom-call(s32[1]{0:T(128)} %bitcast.refs_0_.me_ref, bf16[4,256,192]{2,1,0:T(8,128)(2,1)S(1)} %copy-done.46, bf16[4,256,768]{2,1,0:T(8,128)(2,1)S(1)} %copy-done.45, bf16[4,256,768]{2,1,0:T(8,128)(2,1)} %get-tuple-element.88.fup_ref, ...), custom_call_target="tpu_custom_call" | custom-call | flops 10000000000 | bytes 1048576 | tf_op jit(solution)/shard_map/pallas_call | solution.py:35
  141.0 2.5 slice.273
  146.3 8.3 %shard_map.359 = (bf16[16,96,128]{2,1,0:T(8,128)(2,1)}, bf16[48,4096]{1,0:T(8,128)(2,1)S(1)}, f32[48,4096]{1,0:T(8,128)S(1)}) custom-call(bf16[16,96,128]{2,1,0:T(8,128)(2,1)S(1)} %all-to-all-done.2.g_ref, bf16[48,48]{1,0:T(8,128)(2,1)S(1)} %reshape.220.mix_ref, f32[48,3]{1,0:T(8,128)S(1)} %slice.335.taps_ref, f32[16,48,256]{2,1,0:T(8,128)S(1)} %copy-done.36, ...), custom_call_target="tpu_custom_call" | custom-call | flops 3000000000 | bytes 1048576 | tf_op jit(solution)/shard_map/pallas_call | solution.py:35
  156.3 9.1 %all-to-all-start.3 = ((bf16[16,96,128]{2,1,0:T(8,128)(2,1)}), bf16[16,96,128]{2,1,0:T(8,128)(2,1)S(1)}, u32[]{:S(2)}, u32[]{:S(2)}) async-start(bf16[16,96,128]{2,1,0:T(8,128)(2,1)} %get-tuple-element.66), calls=%async_computation.3 | async-start | bytes 786432 | tf_op jit(solution)/shard_map/all_to_all | solution.py:947
  171.0 14.2 %shard_map.362 = (f32[136,128]{1,0:T(8,128)S(1)}, f32[56,128]{1,0:T(8,128)S(1)}) custom-call(bf16[16,96,128]{2,1,0:T(8,128)(2,1)S(1)} %all-to-all-done.2.g_ref, bf16[16,96,128]{2,1,0:T(8,128)(2,1)S(1)} %copy-done.40, bf16[16,96,128]{2,1,0:T(8,128)(2,1)S(1)} %all-to-all-done.sect_ref, bf16[48,4096]{1,0:T(8,128)(2,1)S(1)} %copy-done.42, ...), custom_call_target="tpu_custom_call" | custom-call | flops 5000000000 | bytes 1048576 | tf_op jit(solution)/shard_map/pallas_call | solution.py:35
  196.7 2.8 shard_map.361
  199.5 4.8 %all-to-all-start.4 = ((bf16[32,32,192]{2,1,0:T(8,128)(2,1)}), bf16[32,32,192]{2,1,0:T(8,128)(2,1)S(1)}, u32[]{:S(2)}, u32[]{:S(2)}) async-start(bf16[32,32,192]{2,1,0:T(8,128)(2,1)} %get-tuple-element.75), calls=%async_computation.4 | async-start | bytes 1048576 | tf_op jit(solution)/shard_map/all_to_all | solution.py:978
  209.5 8.0 %collective-permute-done.11 = bf16[4,24,1408]{2,1,0:T(8,128)(2,1)S(1)} collective-permute-done((bf16[4,24,1408]{2,1,0:T(8,128)(2,1)S(1)}, bf16[4,24,1408]{2,1,0:T(8,128)(2,1)S(1)}, u32[]{:S(2)}, u32[]{:S(2)}) %collective-permute-start.11) | collective-permute-done | bytes 270368 | tf_op jit(solution)/shard_map/ppermute | solution.py:749
  220.8 2.1 collective-permute-done.12
  222.9 2.4 collective-permute-start.13
  225.8 2.4 collective-permute-start.25
  228.9 3.3 %collective-permute-done.25 = bf16[1,24,1408]{2,1,0:T(8,128)(2,1)S(1)} collective-permute-done((bf16[1,24,1408]{2,1,0:T(8,128)(2,1)S(1)}, bf16[1,24,1408]{2,1,0:T(8,128)(2,1)S(1)}, u32[]{:S(2)}, u32[]{:S(2)}) %collective-permute-start.25) | collective-permute-done | bytes 67616 | tf_op jit(solution)/shard_map/ppermute | solution.py:745
  235.6 3.5 %collective-permute-start.16 = (f32[210,128]{1,0:T(8,128)S(1)}, f32[210,128]{1,0:T(8,128)S(1)}, u32[]{:S(2)}, u32[]{:S(2)}) collective-permute-start(f32[210,128]{1,0:T(8,128)S(1)} %pad_maximum_fusion.2), channel_id=1, source_target_pairs={{0,16},{2,18},{4,20},{6,22},{8,24},{10,26},{12,28},{14,30},{16,0},... | collective-permute-start | bytes 322568 | tf_op jit(solution)/shard_map/ppermute | solution.py:745
  239.3 3.0 %collective-permute-done.16 = f32[210,128]{1,0:T(8,128)S(1)} collective-permute-done((f32[210,128]{1,0:T(8,128)S(1)}, f32[210,128]{1,0:T(8,128)S(1)}, u32[]{:S(2)}, u32[]{:S(2)}) %collective-permute-start.16) | collective-permute-done | bytes 107552 | tf_op jit(solution)/shard_map/ppermute | solution.py:745
  242.3 3.5 %collective-permute-done.17 = f32[210,128]{1,0:T(8,128)S(1)} collective-permute-done((f32[210,128]{1,0:T(8,128)S(1)}, f32[210,128]{1,0:T(8,128)S(1)}, u32[]{:S(2)}, u32[]{:S(2)}) %collective-permute-start.17) | collective-permute-done | bytes 107552 | tf_op jit(solution)/shard_map/ppermute | solution.py:745
  248.2 3.5 %collective-permute-start.19 = (f32[432,128]{1,0:T(8,128)S(1)}, f32[432,128]{1,0:T(8,128)S(1)}, u32[]{:S(2)}, u32[]{:S(2)}) collective-permute-start(f32[432,128]{1,0:T(8,128)S(1)} %concatenate.65), channel_id=1, source_target_pairs={{0,2},{2,0},{4,6},{6,4},{8,10},{10,8},{12,14},{14,12},{16,18},{18,... | collective-permute-start | bytes 663560 | tf_op jit(solution)/shard_map/ppermute | solution.py:745
  253.2 6.7 %collective-permute-done.20 = f32[432,128]{1,0:T(8,128)S(1)} collective-permute-done((f32[432,128]{1,0:T(8,128)S(1)}, f32[432,128]{1,0:T(8,128)S(1)}, u32[]{:S(2)}, u32[]{:S(2)}) %collective-permute-start.20) | collective-permute-done | bytes 221216 | tf_op jit(solution)/shard_map/ppermute | solution.py:745
  (356 shorter events, 90.4 us)
Async XLA Ops:
  7.2 78.6 %all-gather.2.cloned.1.call-start = ((), (), s32[]{:S(2)}) async-start(), calls=%async_computation.5 | async-start | bytes 4257792 | tf_op jit(solution)/shard_map/all_gather | solution.py:810
  11.2 9.5 %collective-permute-start = (bf16[24,192]{1,0:T(8,128)(2,1)S(1)}, bf16[24,192]{1,0:T(8,128)(2,1)S(1)}, u32[]{:S(2)}, u32[]{:S(2)}) collective-permute-start(bf16[24,192]{1,0:T(8,128)(2,1)S(1)} %get-tuple-element.143), channel_id=1, source_target_pairs={{0,8},{2,10},{4,12},{6,14},{8,0},{10,2},{12,4},{14,6},{16,24},{18,... | collective-permute-start | bytes 27656 | tf_op jit(solution)/shard_map/ppermute | solution.py:745
  13.4 7.3 %collective-permute-start.1 = (bf16[24,192]{1,0:T(8,128)(2,1)S(1)}, bf16[24,192]{1,0:T(8,128)(2,1)S(1)}, u32[]{:S(2)}, u32[]{:S(2)}) collective-permute-start(bf16[24,192]{1,0:T(8,128)(2,1)S(1)} %get-tuple-element.143), channel_id=1, source_target_pairs={{0,16},{2,18},{4,20},{6,22},{8,24},{10,26},{12,28},{14,30},{16,0},... | collective-permute-start | bytes 27656 | tf_op jit(solution)/shard_map/ppermute | solution.py:745
  15.7 5.0 %collective-permute-start.2 = (bf16[24,192]{1,0:T(8,128)(2,1)S(1)}, bf16[24,192]{1,0:T(8,128)(2,1)S(1)}, u32[]{:S(2)}, u32[]{:S(2)}) collective-permute-start(bf16[24,192]{1,0:T(8,128)(2,1)S(1)} %get-tuple-element.143), channel_id=1, source_target_pairs={{0,24},{2,26},{4,28},{6,30},{8,16},{10,18},{12,20},{14,22},{16,8},... | collective-permute-start | bytes 27656 | tf_op jit(solution)/shard_map/ppermute | solution.py:745
  15.7 16.0 %collective-permute-start.7 = (bf16[2,2,768]{2,1,0:T(2,128)(2,1)S(1)}, bf16[2,2,768]{2,1,0:T(2,128)(2,1)S(1)}, u32[]{:S(2)}, u32[]{:S(2)}) collective-permute-start(bf16[2,2,768]{2,1,0:T(2,128)(2,1)S(1)} %slice.253), channel_id=1, source_target_pairs={{0,2},{2,4},{4,6},{6,8},{8,10},{10,12},{12,14},{14,16},{16,18},{18... | collective-permute-start | bytes 18440 | tf_op jit(solution)/shard_map/ppermute | solution.py:815
  20.7 3.0 %collective-permute-start.3 = (bf16[4,24,192]{2,1,0:T(8,128)(2,1)S(1)}, bf16[4,24,192]{2,1,0:T(8,128)(2,1)S(1)}, u32[]{:S(2)}, u32[]{:S(2)}) collective-permute-start(bf16[4,24,192]{2,1,0:T(8,128)(2,1)S(1)} %pad_maximum_fusion.6), channel_id=1, source_target_pairs={{0,4},{2,6},{4,0},{6,2},{8,12},{10,14},{12,8},{14,10},{16,20},{18,... | collective-permute-start | bytes 110600 | tf_op jit(solution)/shard_map/ppermute | solution.py:745
  21.3 3.1 %collective-permute-start.4 = (bf16[4,24,192]{2,1,0:T(8,128)(2,1)S(1)}, bf16[4,24,192]{2,1,0:T(8,128)(2,1)S(1)}, u32[]{:S(2)}, u32[]{:S(2)}) collective-permute-start(bf16[4,24,192]{2,1,0:T(8,128)(2,1)S(1)} %pad_maximum_fusion.6), channel_id=1, source_target_pairs={{0,1},{1,0},{2,3},{3,2},{4,5},{5,4},{6,7},{7,6},{8,9},{9,8},{10,11... | collective-permute-start | bytes 110600 | tf_op jit(solution)/shard_map/ppermute | solution.py:749
  22.5 5.1 %collective-permute-start.5 = (bf16[4,24,192]{2,1,0:T(8,128)(2,1)S(1)}, bf16[4,24,192]{2,1,0:T(8,128)(2,1)S(1)}, u32[]{:S(2)}, u32[]{:S(2)}) collective-permute-start(bf16[4,24,192]{2,1,0:T(8,128)(2,1)S(1)} %pad_maximum_fusion.6), channel_id=1, source_target_pairs={{0,5},{1,4},{2,7},{3,6},{4,1},{5,0},{6,3},{7,2},{8,13},{9,12},{10,... | collective-permute-start | bytes 110600 | tf_op jit(solution)/shard_map/ppermute | solution.py:753
  27.6 4.6 %collective-permute-start.6 = (bf16[16,24,192]{2,1,0:T(8,128)(2,1)S(1)}, bf16[16,24,192]{2,1,0:T(8,128)(2,1)S(1)}, u32[]{:S(2)}, u32[]{:S(2)}) collective-permute-start(bf16[16,24,192]{2,1,0:T(8,128)(2,1)S(1)} %constant_dynamic-update-slice_fusion.refs_1_), channel_id=1, source_target_pairs={{0,2},{2,0},{4,6},{6,4},{8,10},{10,8},{12,14},{14,12},{16,18},{18,... | collective-permute-start | bytes 442376 | tf_op jit(solution)/shard_map/ppermute | solution.py:745
  36.4 19.4 %all-to-all-start = ((bf16[16,96,128]{2,1,0:T(8,128)(2,1)}), bf16[16,96,128]{2,1,0:T(8,128)(2,1)S(1)}, u32[]{:S(2)}, u32[]{:S(2)}) async-start(bf16[16,96,128]{2,1,0:T(8,128)(2,1)} %get-tuple-element.59), calls=%async_computation | async-start | bytes 786432 | tf_op jit(solution)/shard_map/all_to_all | solution.py:851
  64.9 25.8 %all-to-all-start.1 = ((bf16[16,96,128]{2,1,0:T(8,128)(2,1)}), bf16[16,96,128]{2,1,0:T(8,128)(2,1)}, u32[]{:S(2)}, u32[]{:S(2)}) async-start(bf16[16,96,128]{2,1,0:T(8,128)(2,1)} %get-tuple-element.61), calls=%async_computation.1 | async-start | bytes 786432 | tf_op jit(solution)/shard_map/all_to_all | solution.py:866
  114.0 31.1 %all-to-all-start.2 = ((bf16[16,96,128]{2,1,0:T(8,128)(2,1)}), bf16[16,96,128]{2,1,0:T(8,128)(2,1)S(1)}, u32[]{:S(2)}, u32[]{:S(2)}) async-start(bf16[16,96,128]{2,1,0:T(8,128)(2,1)} %get-tuple-element.65), calls=%async_computation.2 | async-start | bytes 786432 | tf_op jit(solution)/shard_map/all_to_all | solution.py:892
  118.9 5.0 %collective-permute-start.8 = (bf16[4,2,2,192]{3,2,1,0:T(2,128)(2,1)S(1)}, bf16[4,2,2,192]{3,2,1,0:T(2,128)(2,1)S(1)}, u32[]{:S(2)}, u32[]{:S(2)}) collective-permute-start(bf16[4,2,2,192]{3,2,1,0:T(2,128)(2,1)S(1)} %slice.343), channel_id=1, source_target_pairs={{2,0},{4,2},{6,4},{8,6},{10,8},{12,10},{14,12},{16,14},{18,16},{20... | collective-permute-start | bytes 18440 | tf_op jit(solution)/shard_map/ppermute | solution.py:895
  143.5 41.7 %collective-permute-start.9 = (bf16[16,24,1408]{2,1,0:T(8,128)(2,1)}, bf16[16,24,1408]{2,1,0:T(8,128)(2,1)}, u32[]{:S(2)}, u32[]{:S(2)}) collective-permute-start(bf16[16,24,1408]{2,1,0:T(8,128)(2,1)} %slice.273), channel_id=1, source_target_pairs={{0,2},{2,0},{4,6},{6,4},{8,10},{10,8},{12,14},{14,12},{16,18},{18,... | collective-permute-start | bytes 3244040 | tf_op jit(solution)/shard_map/ppermute | solution.py:745
  144.7 44.4 %collective-permute-start.21 = (bf16[16,24,1408]{2,1,0:T(8,128)(2,1)}, bf16[16,24,1408]{2,1,0:T(8,128)(2,1)}, u32[]{:S(2)}, u32[]{:S(2)}) collective-permute-start(bf16[16,24,1408]{2,1,0:T(8,128)(2,1)} %slice.306), channel_id=1, source_target_pairs={{0,2},{2,0},{4,6},{6,4},{8,10},{10,8},{12,14},{14,12},{16,18},{18,... | collective-permute-start | bytes 3244040 | tf_op jit(solution)/shard_map/ppermute | solution.py:745
  156.3 36.5 %all-to-all-start.3 = ((bf16[16,96,128]{2,1,0:T(8,128)(2,1)}), bf16[16,96,128]{2,1,0:T(8,128)(2,1)S(1)}, u32[]{:S(2)}, u32[]{:S(2)}) async-start(bf16[16,96,128]{2,1,0:T(8,128)(2,1)} %get-tuple-element.66), calls=%async_computation.3 | async-start | bytes 786432 | tf_op jit(solution)/shard_map/all_to_all | solution.py:947
  187.7 16.6 %collective-permute-start.10 = (bf16[8,24,1408]{2,1,0:T(8,128)(2,1)}, bf16[8,24,1408]{2,1,0:T(8,128)(2,1)}, u32[]{:S(2)}, u32[]{:S(2)}) collective-permute-start(bf16[8,24,1408]{2,1,0:T(8,128)(2,1)} %slice.346), channel_id=1, source_target_pairs={{0,4},{2,6},{4,0},{6,2},{8,12},{10,14},{12,8},{14,10},{16,20},{18,... | collective-permute-start | bytes 1622024 | tf_op jit(solution)/shard_map/ppermute | solution.py:745
  191.8 15.2 %collective-permute-start.22 = (bf16[8,24,1408]{2,1,0:T(8,128)(2,1)}, bf16[8,24,1408]{2,1,0:T(8,128)(2,1)}, u32[]{:S(2)}, u32[]{:S(2)}) collective-permute-start(bf16[8,24,1408]{2,1,0:T(8,128)(2,1)} %slice.376), channel_id=1, source_target_pairs={{0,1},{1,0},{2,3},{3,2},{4,5},{5,4},{6,7},{7,6},{8,9},{9,8},{10,11... | collective-permute-start | bytes 1622024 | tf_op jit(solution)/shard_map/ppermute | solution.py:749
  199.5 39.7 %all-to-all-start.4 = ((bf16[32,32,192]{2,1,0:T(8,128)(2,1)}), bf16[32,32,192]{2,1,0:T(8,128)(2,1)S(1)}, u32[]{:S(2)}, u32[]{:S(2)}) async-start(bf16[32,32,192]{2,1,0:T(8,128)(2,1)} %get-tuple-element.75), calls=%async_computation.4 | async-start | bytes 1048576 | tf_op jit(solution)/shard_map/all_to_all | solution.py:978
  205.6 11.9 %collective-permute-start.11 = (bf16[4,24,1408]{2,1,0:T(8,128)(2,1)S(1)}, bf16[4,24,1408]{2,1,0:T(8,128)(2,1)S(1)}, u32[]{:S(2)}, u32[]{:S(2)}) collective-permute-start(bf16[4,24,1408]{2,1,0:T(8,128)(2,1)S(1)} %slice.348), channel_id=1, source_target_pairs={{0,1},{1,0},{2,3},{3,2},{4,5},{5,4},{6,7},{7,6},{8,9},{9,8},{10,11... | collective-permute-start | bytes 811016 | tf_op jit(solution)/shard_map/ppermute | solution.py:749
  208.3 11.4 %collective-permute-start.23 = (bf16[4,24,1408]{2,1,0:T(8,128)(2,1)S(1)}, bf16[4,24,1408]{2,1,0:T(8,128)(2,1)S(1)}, u32[]{:S(2)}, u32[]{:S(2)}) collective-permute-start(bf16[4,24,1408]{2,1,0:T(8,128)(2,1)S(1)} %slice.378), channel_id=1, source_target_pairs={{0,4},{2,6},{4,0},{6,2},{8,12},{10,14},{12,8},{14,10},{16,20},{18,... | collective-permute-start | bytes 811016 | tf_op jit(solution)/shard_map/ppermute | solution.py:745
  217.6 5.3 %collective-permute-start.12 = (bf16[2,24,1408]{2,1,0:T(8,128)(2,1)S(1)}, bf16[2,24,1408]{2,1,0:T(8,128)(2,1)S(1)}, u32[]{:S(2)}, u32[]{:S(2)}) collective-permute-start(bf16[2,24,1408]{2,1,0:T(8,128)(2,1)S(1)} %slice.350), channel_id=1, source_target_pairs={{0,8},{2,10},{4,12},{6,14},{8,0},{10,2},{12,4},{14,6},{16,24},{18,... | collective-permute-start | bytes 405512 | tf_op jit(solution)/shard_map/ppermute | solution.py:745
  219.7 6.1 %collective-permute-start.24 = (bf16[2,24,1408]{2,1,0:T(8,128)(2,1)S(1)}, bf16[2,24,1408]{2,1,0:T(8,128)(2,1)S(1)}, u32[]{:S(2)}, u32[]{:S(2)}) collective-permute-start(bf16[2,24,1408]{2,1,0:T(8,128)(2,1)S(1)} %slice.380), channel_id=1, source_target_pairs={{0,8},{2,10},{4,12},{6,14},{8,0},{10,2},{12,4},{14,6},{16,24},{18,... | collective-permute-start | bytes 405512 | tf_op jit(solution)/shard_map/ppermute | solution.py:745
  222.9 5.3 %collective-permute-start.13 = (bf16[1,24,1408]{2,1,0:T(8,128)(2,1)S(1)}, bf16[1,24,1408]{2,1,0:T(8,128)(2,1)S(1)}, u32[]{:S(2)}, u32[]{:S(2)}) collective-permute-start(bf16[1,24,1408]{2,1,0:T(8,128)(2,1)S(1)} %slice.352), channel_id=1, source_target_pairs={{0,16},{2,18},{4,20},{6,22},{8,24},{10,26},{12,28},{14,30},{16,0},... | collective-permute-start | bytes 202760 | tf_op jit(solution)/shard_map/ppermute | solution.py:745
  225.8 6.4 %collective-permute-start.25 = (bf16[1,24,1408]{2,1,0:T(8,128)(2,1)S(1)}, bf16[1,24,1408]{2,1,0:T(8,128)(2,1)S(1)}, u32[]{:S(2)}, u32[]{:S(2)}) collective-permute-start(bf16[1,24,1408]{2,1,0:T(8,128)(2,1)S(1)} %slice.382), channel_id=1, source_target_pairs={{0,16},{2,18},{4,20},{6,22},{8,24},{10,26},{12,28},{14,30},{16,0},... | collective-permute-start | bytes 202760 | tf_op jit(solution)/shard_map/ppermute | solution.py:745
  228.3 7.0 %collective-permute-start.14 = (f32[201,128]{1,0:T(8,128)S(1)}, f32[201,128]{1,0:T(8,128)S(1)}, u32[]{:S(2)}, u32[]{:S(2)}) collective-permute-start(f32[201,128]{1,0:T(8,128)S(1)} %pad_maximum_fusion.3), channel_id=1, source_target_pairs={{0,1},{1,0},{2,3},{3,2},{4,5},{5,4},{6,7},{7,6},{8,9},{9,8},{10,11... | collective-permute-start | bytes 308744 | tf_op jit(solution)/shard_map/ppermute | solution.py:749
  235.3 3.9 %collective-permute-start.15 = (f32[210,128]{1,0:T(8,128)S(1)}, f32[210,128]{1,0:T(8,128)S(1)}, u32[]{:S(2)}, u32[]{:S(2)}) collective-permute-start(f32[210,128]{1,0:T(8,128)S(1)} %pad_maximum_fusion.2), channel_id=1, source_target_pairs={{0,8},{2,10},{4,12},{6,14},{8,0},{10,2},{12,4},{14,6},{16,24},{18,... | collective-permute-start | bytes 322568 | tf_op jit(solution)/shard_map/ppermute | solution.py:745
  235.6 6.7 %collective-permute-start.16 = (f32[210,128]{1,0:T(8,128)S(1)}, f32[210,128]{1,0:T(8,128)S(1)}, u32[]{:S(2)}, u32[]{:S(2)}) collective-permute-start(f32[210,128]{1,0:T(8,128)S(1)} %pad_maximum_fusion.2), channel_id=1, source_target_pairs={{0,16},{2,18},{4,20},{6,22},{8,24},{10,26},{12,28},{14,30},{16,0},... | collective-permute-start | bytes 322568 | tf_op jit(solution)/shard_map/ppermute | solution.py:745
  239.1 6.7 %collective-permute-start.17 = (f32[210,128]{1,0:T(8,128)S(1)}, f32[210,128]{1,0:T(8,128)S(1)}, u32[]{:S(2)}, u32[]{:S(2)}) collective-permute-start(f32[210,128]{1,0:T(8,128)S(1)} %pad_maximum_fusion.2), channel_id=1, source_target_pairs={{0,24},{2,26},{4,28},{6,30},{8,16},{10,18},{12,20},{14,22},{16,8},... | collective-permute-start | bytes 322568 | tf_op jit(solution)/shard_map/ppermute | solution.py:745
  246.6 6.6 %collective-permute-start.18 = (f32[432,128]{1,0:T(8,128)S(1)}, f32[432,128]{1,0:T(8,128)S(1)}, u32[]{:S(2)}, u32[]{:S(2)}) collective-permute-start(f32[432,128]{1,0:T(8,128)S(1)} %concatenate.65), channel_id=1, source_target_pairs={{0,4},{2,6},{4,0},{6,2},{8,12},{10,14},{12,8},{14,10},{16,20},{18,... | collective-permute-start | bytes 663560 | tf_op jit(solution)/shard_map/ppermute | solution.py:745
  248.2 4.9 %collective-permute-start.19 = (f32[432,128]{1,0:T(8,128)S(1)}, f32[432,128]{1,0:T(8,128)S(1)}, u32[]{:S(2)}, u32[]{:S(2)}) collective-permute-start(f32[432,128]{1,0:T(8,128)S(1)} %concatenate.65), channel_id=1, source_target_pairs={{0,2},{2,0},{4,6},{6,4},{8,10},{10,8},{12,14},{14,12},{16,18},{18,... | collective-permute-start | bytes 663560 | tf_op jit(solution)/shard_map/ppermute | solution.py:745
  251.7 8.1 %collective-permute-start.20 = (f32[432,128]{1,0:T(8,128)S(1)}, f32[432,128]{1,0:T(8,128)S(1)}, u32[]{:S(2)}, u32[]{:S(2)}) collective-permute-start(f32[432,128]{1,0:T(8,128)S(1)} %concatenate.65), channel_id=1, source_target_pairs={{0,6},{2,4},{4,2},{6,0},{8,14},{10,12},{12,10},{14,8},{16,22},{18,... | collective-permute-start | bytes 663560 | tf_op jit(solution)/shard_map/ppermute | solution.py:745
  (71 other events, 361.2 us)
Sparse Core Ops, SparseCore 0:
  11.4 74.2 all-gather.1
